TPU v7x, 256 devices: a whole 4x4x8 slice. The times are simulated.
256 devices in a mesh: replica: 32 (over y, z_lo, core), fsdp: 8 (over z_hi, x).
Axes of the slice: x: 4, y: 4, z: 8 (z_hi: 2, z_lo: 4; z = z_hi * 4 + z_lo), core: 2. Of those that a mesh axis runs over, the one named last changes fastest.
Arguments:
- params: bfloat16 [32, 4608, 1024], P('replica', 'fsdp'), may hold values from -6 to 6
- tokens: bfloat16 [32, 4096, 4608], P('replica', 'fsdp'), may hold values from -6 to 6
- cotangent: bfloat16 [32, 4096, 1024], P('replica', 'fsdp'), may hold values from -0.1875 to 0.1875
- gain: float32 [4608], replicated, may hold values from 0.1 to 1.9
- glob: float32 [4608, 1024], P(('fsdp', 'replica')), may hold values from -6 to 6
- momentum: float32 [4608, 1024], P(('fsdp', 'replica')), may hold values from -4 to 4
- prev_global: float32 [4608, 1024], P(('fsdp', 'replica')), may hold values from -6 to 6
Outputs:
- new_params: bfloat16 [32, 4608, 1024], P('replica', 'fsdp')
- grad_tokens: bfloat16 [32, 4096, 4608], P('replica', 'fsdp')
- new_global: float32 [4608, 1024], P(('fsdp', 'replica'))
- new_momentum: float32 [4608, 1024], P(('fsdp', 'replica'))
All inputs are finite; a program needn't handle non-finite values.
Results may differ from a plain program's by a relative error of at most 0.014.
Values may be sent and summed in bfloat16 or wider, within the bound.
A program may use at most 128 MiB of HBM per device.

v0:
```python
import jax
import jax.numpy as jnp
from jax import lax
from jax.sharding import PartitionSpec as P

inner_rate = 0.5
outer_rate = 0.7
nesterov = 0.9
mix_weight = 0.5
eps = 1e-06


def shards(params, tokens, cotangent, gain, glob, momentum, prev_global):
    weights = params[0]
    x = tokens[0].astype(jnp.float32)
    values_grad = cotangent[0]
    inv = lax.rsqrt(jnp.mean(x * x, axis=-1, keepdims=True) + eps)
    unit = x * inv
    normed = (unit * gain).astype(jnp.bfloat16)
    grad = lax.psum_scatter(
        lax.dot_general(
            normed, values_grad, (((0,), (0,)), ((), ())), preferred_element_type=jnp.float32
        ).astype(jnp.bfloat16),
        "fsdp",
        scatter_dimension=0,
        tiled=True,
    ).astype(jnp.float32)
    updated = (weights.astype(jnp.float32) - inner_rate * grad).astype(jnp.bfloat16)
    dn = lax.dot_general(
        values_grad,
        lax.all_gather(weights, "fsdp", axis=0, tiled=True),
        (((1,), (1,)), ((), ())),
        preferred_element_type=jnp.float32,
    )
    scaled = gain * dn
    grad_tokens = (inv * (scaled - unit * jnp.mean(unit * scaled, axis=-1, keepdims=True))).astype(
        jnp.bfloat16
    )
    share = glob.shape[0]
    replica_pos = lax.axis_index("replica")
    replica_count = lax.axis_size("replica")
    wide = updated.astype(jnp.float32)
    total = lax.psum(wide, "replica")
    mine = lax.dynamic_slice_in_dim(total, replica_pos * share, share, 0)
    avg = mine / replica_count
    delta = glob - avg
    new_momentum = nesterov * momentum + delta
    new_global = glob - outer_rate * (delta + nesterov * new_momentum)
    arrived = lax.all_gather(prev_global, "replica", axis=0, tiled=True)
    mixed = ((1.0 - mix_weight) * wide + mix_weight * arrived).astype(jnp.bfloat16)
    return (mixed[None], grad_tokens[None], new_global, new_momentum)


def solution(mesh):
    placed = (
        P("replica", "fsdp", None),
        P("replica", "fsdp", None),
        P("replica", "fsdp", None),
        P(),
        P(("fsdp", "replica"), None),
        P(("fsdp", "replica"), None),
        P(("fsdp", "replica"), None),
    )
    return jax.shard_map(
        shards,
        mesh=mesh,
        in_specs=placed,
        out_specs=(
            P("replica", "fsdp", None),
            P("replica", "fsdp", None),
            P(("fsdp", "replica"), None),
            P(("fsdp", "replica"), None),
        ),
        check_vma=False,
    )
```

profile of v0, /device:TPU:1, one launch (start us, length us, event | category | flops | bytes accessed | tf_op | source)
XLA Modules:
  0.0 676.2 jit_solution(7583203926531277895)
XLA Ops:
  8.0 0.0 copy-start
  8.0 0.0 all-gather.7.cloned.1.call-start
  8.1 0.7 all-gather.7.cloned.1.call-update
  8.7 0.0 reduce-scatter.2.cloned.1.call-start
  8.8 3.3 fusion.8
  12.1 0.0 copy-done
  12.2 10.2 %convolution_convert_fusion = bf16[4608,1024]{1,0:T(8,128)(2,1)} fusion(bf16[1,512,4608]{2,1,0:T(8,128)(2,1)} %param.8, f32[4608]{0:T(1024)} %param.10, f32[512]{0:T(512)S(1)} %add_rsqrt_fusion, bf16[1,512,1024]{2,1,0:T(8,128)(2,1)S(1)} %copy-done), kind=kOutput, calls=%fused_computation.6 | convolution fusion | flops 4845993984 | bytes 15224832 | tf_op jit(solution)/shard_map/dot_general | solution.py:21
  22.3 0.0 reduce-scatter.2.cloned.1.call-update
  22.4 0.0 copy-start.3
  22.4 0.0 all-gather.5.cloned.1.call-start
  22.4 0.7 all-gather.5.cloned.1.call-update
  23.1 0.0 all-reduce.2.cloned.1.call-start
  23.2 139.7 %all-gather.7.cloned.1.call-done = f32[32,18,1024]{2,1,0:T(8,128)} async-done(((f32[1,18,1024]{2,1,0:T(8,128)}), f32[32,18,1024]{2,1,0:T(8,128)}) %all-gather.7.cloned.1.call-update) | async-done | bytes 2359312 | tf_op jit(solution)/shard_map/all_gather | solution.py:49
  162.9 2.0 reshape.41
  164.9 55.8 %reduce-scatter.2.cloned.1.call-done = bf16[576,1024]{1,0:T(8,128)(2,1)} async-done(((bf16[4608,1024]{1,0:T(8,128)(2,1)}), bf16[576,1024]{1,0:T(8,128)(2,1)}) %reduce-scatter.2.cloned.1.call-update) | async-done | bytes 1179664 | tf_op jit(solution)/shard_map/reduce_scatter | solution.py:20
  220.8 4.1 fusion.20
  224.8 0.0 all-reduce.2.cloned.1.call-update
  224.9 160.0 %all-gather.5.cloned.1.call-done = bf16[1,4608,1024]{2,1,0:T(8,128)(2,1)} async-done(((bf16[1,576,1024]{2,1,0:T(8,128)(2,1)}), bf16[1,4608,1024]{2,1,0:T(8,128)(2,1)}) %all-gather.5.cloned.1.call-update) | async-done | bytes 9437200 | tf_op jit(solution)/shard_map/all_gather | solution.py:31
  384.9 0.0 copy-done.3
  384.9 12.4 %fusion.4 = (f32[512]{0:T(512)S(1)}, f32[512,4608]{1,0:T(8,128)}) fusion(bf16[1,512,4608]{2,1,0:T(8,128)(2,1)} %param.8, f32[4608]{0:T(1024)S(1)} %copy-done.3, f32[512]{0:T(512)S(1)} %add_rsqrt_fusion, bf16[1,4608,1024]{2,1,0:T(8,128)(2,1)} %all-gather.5.cloned.1.call-done, bf16[1,512,1024]{2,1,0:T(8,128)(2,1)S(1)} %copy-done), kind=kOutput, calls=%fused_computation.7 | convolution fusion | flops 4843634176 | bytes 24664064 | tf_op jit(solution)/shard_map/dot_general | solution.py:29
  397.2 0.0 copy-start.1
  397.3 0.0 copy-start.2
  397.3 10.3 %fusion.15 = bf16[1,512,4608]{2,1,0:T(8,128)(2,1)} fusion(bf16[1,512,4608]{2,1,0:T(8,128)(2,1)} %param.8, f32[512,4608]{1,0:T(8,128)} %get-tuple-element.9, f32[512]{0:T(512)S(1)} %broadcast_multiply_fusion, f32[4608]{0:T(1024)S(1)} %copy-done.3, f32[512]{0:T(512)S(1)} %add_rsqrt_fusion), kind=kLoop, calls=%fused_computation.17 | loop fusion | flops 16515072 | bytes 18896896 | tf_op jit(solution)/shard_map/broadcast_in_dim | solution.py:51
  407.5 259.9 %all-reduce.2.cloned.1.call-done = f32[576,1024]{1,0:T(8,128)} async-done(((f32[576,1024]{1,0:T(8,128)}), f32[576,1024]{1,0:T(8,128)}) %all-reduce.2.cloned.1.call-update) | async-done | bytes 2359312 | tf_op jit(solution)/shard_map/psum | solution.py:43
  667.5 0.0 copy-done.1
  667.5 0.0 copy-done.2
  667.5 1.6 multiply_subtract_fusion
  (2 shorter events, 0.0 us)
Async XLA Ops:
  8.0 4.1 copy-start
  8.0 154.9 %all-gather.7.cloned.1.call-start = ((), (), s32[]{:S(2)}) async-start(), calls=%async_computation.4 | async-start | bytes 3244032 | tf_op jit(solution)/shard_map/all_gather | solution.py:49
  8.7 212.0 %reduce-scatter.2.cloned.1.call-start = ((), (), s32[]{:S(2)}) async-start(), calls=%async_computation.1 | async-start | bytes 10616832 | tf_op jit(solution)/shard_map/reduce_scatter | solution.py:20
  22.4 362.5 %copy-start.3 = (f32[4608]{0:T(1024)S(1)}, f32[4608]{0:T(1024)}, u32[]{:S(2)}) copy-start(f32[4608]{0:T(1024)} %param.10) | copy-start | bytes 55300
  22.4 362.5 %all-gather.5.cloned.1.call-start = ((), (), s32[]{:S(2)}) async-start(), calls=%async_computation.3 | async-start | bytes 10616832 | tf_op jit(solution)/shard_map/all_gather | solution.py:31
  23.1 644.3 %all-reduce.2.cloned.1.call-start = ((), (), s32[]{:S(2)}) async-start(), calls=%async_computation.2 | async-start | bytes 4718592 | tf_op jit(solution)/shard_map/psum | solution.py:43
  397.2 270.2 %copy-start.1 = (f32[18,1024]{1,0:T(8,128)S(1)}, f32[18,1024]{1,0:T(8,128)}, u32[]{:S(2)}) copy-start(f32[18,1024]{1,0:T(8,128)} %param.11) | copy-start | bytes 221188
  397.3 270.2 %copy-start.2 = (f32[18,1024]{1,0:T(8,128)S(1)}, f32[18,1024]{1,0:T(8,128)}, u32[]{:S(2)}) copy-start(f32[18,1024]{1,0:T(8,128)} %param.12) | copy-start | bytes 221188
Sparse Core Ops, SparseCore 0:
  10.9 151.9 all-gather.6
  165.8 219.0 all-gather.4
  387.7 279.7 all-reduce.1
Sparse Core Ops, SparseCore 1:
  22.4 198.3 reduce-scatter.1
where the time goes:
time: 676 us
  waiting for transfers between devices  617 us (91%)
  matrix products  22.6 us (3%)
  other arithmetic  19.3 us (3%)
  between operations  15.2 us (2%)
    psum x1, waiting for transfers between devices, shards(): total = lax.psum(wide, 'replica')  260 us
    all_gather x1, waiting for transfers between devices, shards(): lax.all_gather(weights, 'fsdp', axis=0, tiled=True)  160 us
    all_gather x1, waiting for transfers between devices, shards(): arrived = lax.all_gather(prev_global, 'replica', axis=0, tiled=True)  140 us
    reduce_scatter x1, waiting for transfers between devices, shards(): lax.psum_scatter(lax.dot_general(normed, values_grad, (((0,), (0,)), ((),...  55.8 us
  transfers between devices with their start and end apart: 4, of which 4 were waited for; matrix products, arithmetic and copies ran while one was open for 6% of the time, Pallas kernels for 0%

commit v1 on v0

v1 whole, which is shorter than its diff:
```python
import jax
import jax.numpy as jnp
from jax import lax
from jax.experimental import pallas as pl
from jax.experimental.pallas import tpu as pltpu
from jax.sharding import PartitionSpec as P

inner_rate = 0.5
outer_rate = 0.7
nesterov = 0.9
mix_weight = 0.5
eps = 1e-06

MESH = pl.DeviceIdType.MESH
F32 = jnp.float32
BF16 = jnp.bfloat16

D = 4608
HV = 1024
T = 512
Q = 1152
S = 576
NC = 4
CW = HV // NC
NT = 8
TR = T // NT
NZ = 4
ZR = S // NZ
YR = S // 4
WR = 40
OWN = 18
PZ = 48


def kernel(
    params, tokens, cot, gain, glob, mom, prev,
    new_params, grad_tokens, new_global, new_momentum,
    tok, cc, invb, gb, nst, nnt, wg, gs, gr, gk, zs, zr, up, cr, s2, yr, s8, lr, tot,
    xs, xr, xo, po, pz, pzr, pa, pfull,
    a_s, a_r, b_s, b_r, z_s, z_r, c_s, c_r, y_s, y_r, l_s, l_r, loc, outs,
):
    rep = lax.axis_index("replica")
    fs = lax.axis_index("fsdp")
    core = lax.rem(rep, 2)
    zl = lax.rem(lax.div(rep, 2), 4)
    y = lax.div(rep, 8)
    x = lax.rem(fs, 4)
    zh = lax.div(fs, 4)
    half = lax.div(x, 2)
    par = lax.rem(x, 2)

    dev_a = (rep, zh * 4 + lax.rem(jnp.where(par == 0, x + 3, x + 1), 4))
    dev_b = (rep, zh * 4 + half * 2 + (1 - par))
    dev_z = (rep, (1 - zh) * 4 + x)
    dev_c = ((y * 4 + zl) * 2 + (1 - core), fs)
    dev_y = [((lax.rem(y + d, 4) * 4 + zl) * 2 + core, fs) for d in (1, 2, 3)]
    dev_l = [((y * 4 + lax.rem(zl + d, 4)) * 2 + core, fs) for d in (1, 2, 3)]

    def remote(src, dst, sends, recvs, i, dev):
        return pltpu.make_async_remote_copy(
            src_ref=src,
            dst_ref=dst,
            send_sem=sends.at[i],
            recv_sem=recvs.at[i],
            device_id=dev,
            device_id_type=MESH,
        )

    def column(b):
        plane = (1 - zh) if b % 2 == 0 else zh
        side = (1 - half) if b < 2 else half
        return pl.multiple_of(plane * (D // 2) + side * Q, 128)

    my_rows = pl.multiple_of(par * S, 64)
    its_rows = pl.multiple_of((1 - par) * S, 64)

    loads = [
        pltpu.make_async_copy(tokens.at[:, pl.ds(column(b), Q)], tok.at[b], loc.at[b])
        for b in range(4)
    ]
    load_cot = pltpu.make_async_copy(cot, cc.at[pl.ds(0, T)], loc.at[4])
    load_w = pltpu.make_async_copy(params, wg.at[1, pl.ds(my_rows, S)], loc.at[5])

    barrier = pltpu.get_barrier_semaphore()
    peers = [dev_a, dev_b, dev_z, dev_c] + dev_y + dev_l
    for dev in peers:
        pl.semaphore_signal(barrier, inc=1, device_id=dev, device_id_type=MESH)
    for cp in loads:
        cp.start()
    load_cot.start()
    load_w.start()
    pl.semaphore_wait(barrier, len(peers))

    send_cot = remote(cot, cc.at[pl.ds(T, T)], a_s, a_r, 0, dev_a)
    send_cot.start()
    send_w = remote(params, wg.at[1, pl.ds(my_rows, S)], b_s, b_r, 0, dev_b)
    send_w.start()
    far_w = [
        remote(
            params.at[pl.ds(k * ZR, ZR)],
            wg.at[0, pl.ds(pl.multiple_of(my_rows + k * ZR, 16), ZR)],
            z_s, z_r, k, dev_z,
        )
        for k in range(NZ)
    ]
    for cp in far_w:
        cp.start()
    send_prev = remote(prev, po, c_s, c_r, 0, dev_c)
    send_prev.start()

    for b in range(4):
        gb[b] = gain[:, pl.ds(column(b), Q)]
    for cp in loads:
        cp.wait()

    @pl.loop(0, T // 32)
    def _(i):
        rows = pl.ds(pl.multiple_of(i * 32, 32), 32)
        acc = jnp.zeros((32, 128), F32)
        for b in range(4):
            for j in range(Q // 128):
                v = tok[b, rows, j * 128 : (j + 1) * 128].astype(F32)
                acc = acc + v * v
        inv = lax.rsqrt(jnp.sum(acc, axis=-1, keepdims=True) * (1.0 / D) + eps)
        invb[rows, :] = jnp.broadcast_to(inv, (32, 128))

    def normed(b, put):
        @pl.loop(0, Q // 128)
        def _(j):
            cols = pl.ds(pl.multiple_of(j * 128, 128), 128)
            v = tok[b, :, cols].astype(F32) * invb[...] * gb[b, :, cols]
            put(cols, v.T.astype(BF16))

    def put_send(o):
        def put(rows, v):
            nst[o, rows, :] = v
        return put

    def put_own(o):
        def put(rows, v):
            nnt[o, rows, 0:T] = v
        return put

    send_n = []
    for o in range(2):
        normed(o, put_send(o))
        for p, start in enumerate((my_rows, its_rows)):
            rows = pl.ds(start, S)
            cp = remote(nst.at[o, rows], nnt.at[o, rows, pl.ds(T, T)], a_s, a_r, 1 + 2 * o + p, dev_a)
            cp.start()
            send_n.append(cp)

    send_prev.wait_recv()
    wide = pl.ds(pl.multiple_of(core * (HV // 2), 128), HV // 2)
    pz[...] = jnp.zeros_like(pz)

    @pl.when(core == 0)
    def _():
        pz[0:OWN, :] = prev[:, wide]
        pz[OWN : 2 * OWN, :] = po[:, wide]

    @pl.when(core == 1)
    def _():
        pz[0:OWN, :] = po[:, wide]
        pz[OWN : 2 * OWN, :] = prev[:, wide]

    pzr[zl] = pz[...].astype(BF16)
    prev_l = [remote(pzr.at[zl], pzr.at[zl], l_s, l_r, d, dev_l[d]) for d in range(3)]
    for cp in prev_l:
        cp.start()

    for o in range(2):
        normed(2 + o, put_own(o))

    for cp in prev_l:
        cp.wait_recv()
    for k in range(4):
        pa[k * 36 : (k + 1) * 36, :] = pzr[k, 0:36, :].astype(F32)
    y_rows = pl.ds(pl.multiple_of(y * YR, 16), YR)
    pfull[core, y_rows, :] = pa[...].astype(BF16)
    prev_y = [
        remote(pfull.at[core, y_rows], pfull.at[core, y_rows], y_s, y_r, d, dev_y[d])
        for d in range(3)
    ]
    for cp in prev_y:
        cp.start()

    forward = [
        remote(
            wg.at[0, pl.ds(pl.multiple_of(my_rows + k * ZR, 16), ZR)],
            wg.at[0, pl.ds(pl.multiple_of(my_rows + k * ZR, 16), ZR)],
            b_s, b_r, 1 + k, dev_b,
        )
        for k in range(NZ)
    ]

    def pass_on(k):
        far_w[k].wait_recv()
        forward[k].start()

    def send_g(o, c):
        return remote(gs.at[o, c], gr.at[o, c], b_s, b_r, 5 + NC * o + c, dev_b)

    def product(o, rows, c):
        cols = pl.ds(pl.multiple_of(c * CW, 128), CW)
        return jnp.dot(nnt[o, pl.ds(rows, S), :], cc[:, cols], preferred_element_type=F32)

    def give(o):
        send_n[2 * o].wait_recv()

        @pl.loop(0, NC)
        def _(c):
            gs[o, c] = product(o, its_rows, c).astype(BF16)
            send_g(o, c).start()

    def keep(o):
        send_n[2 * o + 1].wait_recv()

        @pl.loop(0, NC)
        def _(c):
            gk[o, c] = product(o, my_rows, c)

    def send_s(c):
        return remote(zs.at[c], zr.at[c], z_s, z_r, NZ + c, dev_z)

    def far_sum(c):
        send_g(0, c).wait_recv()
        zs[c] = (gk[0, c] + gr[0, c].astype(F32)).astype(BF16)
        send_s(c).start()

    pass_on(0)
    for cp in prev_y:
        cp.wait_recv()
    prev_c = remote(pfull.at[core], pfull.at[core], c_s, c_r, 1, dev_c)
    prev_c.start()
    pass_on(1)
    load_cot.wait()
    load_w.wait()
    send_cot.wait_recv()
    give(0)
    pass_on(2)
    keep(0)
    pass_on(3)
    far_sum(0)
    far_sum(1)
    give(1)
    far_sum(2)
    far_sum(3)

    send_w.wait_recv()
    for cp in forward:
        cp.wait_recv()

    def dn(first, put):
        for o in range(2):

            @pl.loop(0, 3)
            def _(n):
                rows = pl.ds(pl.multiple_of(n * 384, 128), 384)
                cols = pl.ds(pl.multiple_of(o * Q + n * 384, 128), 384)
                put(
                    cols,
                    lax.dot_general(
                        cc[first : first + T, :],
                        wg[o, rows, :],
                        (((1,), (1,)), ((), ())),
                        preferred_element_type=F32,
                    ),
                )

    def put_xs(cols, v):
        xs[:, cols] = v.astype(BF16)

    def put_xo(cols, v):
        xo[:, cols] = v

    dn(T, put_xs)
    send_x = []
    for t in range(NT):
        rows = pl.ds(t * TR, TR)
        cp = remote(xs.at[rows], xr.at[rows], a_s, a_r, 5 + t, dev_a)
        cp.start()
        send_x.append(cp)
    keep(1)
    dn(0, put_xo)

    stores = []

    def finish(t):
        send_x[t].wait_recv()

        @pl.loop(0, TR // 16)
        def _(i):
            rows = pl.ds(pl.multiple_of(t * TR + i * 16, 16), 16)
            inv = invb[rows, :]

            def parts(b, j):
                cols = slice(j * 128, (j + 1) * 128)
                unit = tok[b, rows, cols].astype(F32) * inv
                at = (b % 2) * Q + j * 128
                if b < 2:
                    d = xr[rows, at : at + 128].astype(F32)
                else:
                    d = xo[rows, at : at + 128]
                return unit, gb[b, :, cols] * d

            acc = jnp.zeros((16, 128), F32)
            for b in range(4):
                for j in range(Q // 128):
                    unit, scaled = parts(b, j)
                    acc = acc + unit * scaled
            mean = jnp.sum(acc, axis=-1, keepdims=True) * (1.0 / D)
            for b in range(4):
                for j in range(Q // 128):
                    unit, scaled = parts(b, j)
                    tok[b, rows, j * 128 : (j + 1) * 128] = (inv * (scaled - unit * mean)).astype(BF16)

        for b in range(4):
            cp = pltpu.make_async_copy(
                tok.at[b, pl.ds(t * TR, TR)],
                grad_tokens.at[pl.ds(t * TR, TR), pl.ds(column(b), Q)],
                outs.at[t, b],
            )
            cp.start()
            stores.append(cp)

    def send_up(c):
        return remote(up.at[2 * c + 1 - core], cr.at[c], c_s, c_r, 2 + c, dev_c)

    def send_y(c, d):
        rows = pl.ds(pl.multiple_of(lax.rem(y + d + 1, 4) * YR, 16), YR)
        return remote(s2.at[c, rows], yr.at[c, d], y_s, y_r, 3 + 3 * c + d, dev_y[d])

    def window(pos):
        return pl.multiple_of(pos * 36 - lax.rem(pos, 2) * 4, 8)

    def send_l(c, d):
        rows = pl.ds(window(lax.rem(zl + d + 1, 4)), WR)
        return remote(s8.at[c, rows], lr.at[c, d], l_s, l_r, 3 + 3 * c + d, dev_l[d])

    def send_tot(c):
        return remote(tot.at[2 * c + core], tot.at[2 * c + core], c_s, c_r, 6 + c, dev_c)

    def update(c):
        if c == 0:
            prev_c.wait_recv()
        send_g(1, c).wait_recv()
        send_s(c).wait_recv()
        for k in range(2):
            part = slice(k * 128, (k + 1) * 128)
            cols = slice(c * CW + k * 128, c * CW + (k + 1) * 128)
            grad = gk[1, c, :, part] + gr[1, c, :, part].astype(F32) + zr[c, :, part].astype(F32)
            now = (wg[1, pl.ds(my_rows, S), cols].astype(F32) - inner_rate * grad).astype(BF16)
            up[2 * c + k] = now
        send_up(c).start()
        for k in range(2):
            cols = slice(c * CW + k * 128, c * CW + (k + 1) * 128)
            at = (c % 2) * CW + k * 128
            old = pfull[c // 2, :, at : at + 128].astype(F32)
            new_params[:, cols] = (
                (1.0 - mix_weight) * up[2 * c + k].astype(F32) + mix_weight * old
            ).astype(BF16)

    def both_cores(c):
        send_up(c).wait_recv()
        s2[c] = up[2 * c + core].astype(F32) + cr[c].astype(F32)
        for d in range(3):
            send_y(c, d).start()

    def all_y(c):
        for d in range(3):
            send_y(c, d).wait_recv()
        s8[c] = s2[c, y_rows, :] + yr[c, 0] + yr[c, 1] + yr[c, 2]
        for d in range(3):
            send_l(c, d).start()

    def all_l(c):
        for d in range(3):
            send_l(c, d).wait_recv()
        tot[2 * c + core] = s8[c, pl.ds(window(zl), WR), :] + lr[c, 0] + lr[c, 1] + lr[c, 2]
        send_tot(c).start()

    update(0)
    finish(0)
    both_cores(0)
    finish(1)
    all_y(0)
    update(1)
    finish(2)
    all_l(0)
    both_cores(1)
    finish(3)
    all_y(1)
    update(2)
    finish(4)
    all_l(1)
    both_cores(2)
    update(3)
    finish(5)
    all_y(2)
    both_cores(3)
    finish(6)
    all_l(2)
    all_y(3)
    all_l(3)

    for c in range(NC):
        send_tot(c).wait_recv()
    place = lax.rem(zl, 2) * 2 + core
    for j in range(HV // 128):
        cols = slice(j * 128, (j + 1) * 128)
        total = jnp.where(
            place < 2,
            jnp.where(place == 0, tot[j, 0:18, :], tot[j, 18:36, :]),
            jnp.where(place == 2, tot[j, 4:22, :], tot[j, 22:40, :]),
        )
        delta = glob[:, cols] - total * (1.0 / 32)
        moved = nesterov * mom[:, cols] + delta
        new_momentum[:, cols] = moved
        new_global[:, cols] = glob[:, cols] - outer_rate * (delta + nesterov * moved)
    finish(7)

    for cp in [send_cot, send_w, send_prev, prev_c] + far_w + forward + send_n + send_x + prev_l + prev_y:
        cp.wait_send()
    for c in range(NC):
        send_g(0, c).wait_send()
        send_g(1, c).wait_send()
        send_s(c).wait_send()
        send_up(c).wait_send()
        send_tot(c).wait_send()
        for d in range(3):
            send_y(c, d).wait_send()
            send_l(c, d).wait_send()
    for cp in stores:
        cp.wait()


def shards(params, tokens, cotangent, gain, glob, momentum, prev_global):
    vmem = pl.BlockSpec(memory_space=pltpu.VMEM)
    hbm = pl.BlockSpec(memory_space=pl.ANY)
    dma = pltpu.SemaphoreType.DMA
    out = pl.pallas_call(
        kernel,
        out_shape=(
            jax.ShapeDtypeStruct((S, HV), BF16),
            jax.ShapeDtypeStruct((T, D), BF16),
            jax.ShapeDtypeStruct((OWN, HV), F32),
            jax.ShapeDtypeStruct((OWN, HV), F32),
        ),
        in_specs=[hbm, hbm, hbm, vmem, vmem, vmem, vmem],
        out_specs=(vmem, hbm, vmem, vmem),
        scratch_shapes=[
            pltpu.VMEM((4, T, Q), BF16),
            pltpu.VMEM((2 * T, HV), BF16),
            pltpu.VMEM((T, 128), F32),
            pltpu.VMEM((4, 1, Q), F32),
            pltpu.VMEM((2, Q, T), BF16),
            pltpu.VMEM((2, Q, 2 * T), BF16),
            pltpu.VMEM((2, Q, HV), BF16),
            pltpu.VMEM((2, NC, S, CW), BF16),
            pltpu.VMEM((2, NC, S, CW), BF16),
            pltpu.VMEM((2, NC, S, CW), F32),
            pltpu.VMEM((NC, S, CW), BF16),
            pltpu.VMEM((NC, S, CW), BF16),
            pltpu.VMEM((2 * NC, S, 128), BF16),
            pltpu.VMEM((NC, S, 128), BF16),
            pltpu.VMEM((NC, S, 128), F32),
            pltpu.VMEM((NC, 3, YR, 128), F32),
            pltpu.VMEM((NC, YR, 128), F32),
            pltpu.VMEM((NC, 3, WR, 128), F32),
            pltpu.VMEM((2 * NC, WR, 128), F32),
            pltpu.VMEM((T, 2 * Q), BF16),
            pltpu.VMEM((T, 2 * Q), BF16),
            pltpu.VMEM((T, 2 * Q), F32),
            pltpu.VMEM((OWN, HV), F32),
            pltpu.VMEM((PZ, HV // 2), F32),
            pltpu.VMEM((4, PZ, HV // 2), BF16),
            pltpu.VMEM((YR, HV // 2), F32),
            pltpu.VMEM((2, S, HV // 2), BF16),
            dma((5 + NT,)), dma((5 + NT,)),
            dma((5 + 2 * NC,)), dma((5 + 2 * NC,)),
            dma((NZ + NC,)), dma((NZ + NC,)),
            dma((2 + 2 * NC,)), dma((2 + 2 * NC,)),
            dma((3 + 3 * NC,)), dma((3 + 3 * NC,)),
            dma((3 + 3 * NC,)), dma((3 + 3 * NC,)),
            dma((6,)),
            dma((NT, 4)),
        ],
        compiler_params=pltpu.CompilerParams(
            collective_id=0, has_side_effects=True, vmem_limit_bytes=60 * 1024 * 1024
        ),
        cost_estimate=pl.CostEstimate(
            flops=4 * T * D * HV, bytes_accessed=16 * 1024 * 1024, transcendentals=T
        ),
        name="diloco",
    )(params[0], tokens[0], cotangent[0], gain.reshape(1, D), glob, momentum, prev_global)
    return (out[0][None], out[1][None], out[2], out[3])


def solution(mesh):
    placed = (
        P("replica", "fsdp", None),
        P("replica", "fsdp", None),
        P("replica", "fsdp", None),
        P(),
        P(("fsdp", "replica"), None),
        P(("fsdp", "replica"), None),
        P(("fsdp", "replica"), None),
    )
    return jax.shard_map(
        shards,
        mesh=mesh,
        in_specs=placed,
        out_specs=(
            P("replica", "fsdp", None),
            P("replica", "fsdp", None),
            P(("fsdp", "replica"), None),
            P(("fsdp", "replica"), None),
        ),
        check_vma=False,
    )
```

time: 676 us -> 197 us (0.29)
  waiting for transfers between devices: 617 us -> 0 us
  Pallas kernels: 0 us -> 187 us
  matrix products: 22.6 us -> 0 us
  other arithmetic: 19.3 us -> 0 us
  between operations: 15.2 us -> 0.64 us
  local copies, waits for them, and re-layouts: 2.07 us -> 9.86 us
    all_gather x2 -> x0, waiting for transfers between devices: 300 us -> none  [the longest x1 160 us: shards(): lax.all_gather(weights, 'fsdp', axis=0, tiled=True)]
    psum x1 -> x0, waiting for transfers between devices: 260 us -> none  [shards(): total = lax.psum(wide, 'replica')]
    pallas_call x0 -> x1, Pallas kernels: none -> 187 us  [shards(): pl.pallas_call(kernel, out_shape=(jax.ShapeDtypeStruct((S, HV), BF16), ja...]
    reduce_scatter x1 -> x0, waiting for transfers between devices: 55.8 us -> none  [shards(): lax.psum_scatter(lax.dot_general(normed, values_grad, (((0,), (0,)), ((),...]
    dot_general x2 -> x0, matrix products: 22.6 us -> none  [the longest x1 12.4 us: shards(): lax.dot_general(values_grad, lax.all_gather(weights, 'fsdp', axis=0, tile...]
    broadcast_in_dim x1 -> x0, other arithmetic: 10.3 us -> none  [shards(): return (mixed[None], grad_tokens[None], new_global, new_momentum)]
  transfers between devices with their start and end apart: 4 -> 0, of which waited for: 4 -> 0; matrix products, arithmetic and copies ran while one was open for 6% -> 0% of each run, Pallas kernels for 0% -> 0%
where the time goes in v1:
time: 197 us
  Pallas kernels  187 us (95%)
  local copies, waits for them, and re-layouts  9.86 us (5%)
    pallas_call x1, Pallas kernels, shards(): pl.pallas_call(kernel, out_shape=(jax.ShapeDtypeStruct((S, HV), BF16), ja...  187 us
    unnamed x8, local copies, waits for them, and re-layouts  8.52 us

profile of v1, /device:TPU:1, one launch (start us, length us, event | category | flops | bytes accessed | tf_op | source)
XLA Modules:
  0.0 197.1 jit_solution(2802672235904682197)
XLA Ops:
  0.6 1.3 reshape.11.gain
  2.0 186.6 %diloco.1 = (bf16[576,1024]{1,0:T(8,128)(2,1)}, bf16[512,4608]{1,0:T(8,128)(2,1)}, f32[18,1024]{1,0:T(8,128)}, f32[18,1024]{1,0:T(8,128)}) custom-call(bf16[576,1024]{1,0:T(8,128)(2,1)} %bitcast.8, bf16[512,4608]{1,0:T(8,128)(2,1)} %bitcast.7, bf16[512,1024]{1,0:T(8,128)(2,1)} %bitcast.9, f32[1,4608]{1,0:T(1,128)} %reshape.11.gain, f32[18,1024]{1,0:T(8,128)} %glob.1, ...), custom_call_target="tpu_custom_call" | custom-call | flops 9663676416 | bytes 16777216 | tf_op jit(solution)/shard_map/diloco/pallas_call | solution.py:442
  188.6 2.4 %copy.15 = bf16[1,576,1024]{2,1,0:T(8,128)(2,1)} copy(bf16[1,576,1024]{2,1,0:T(8,128)(2,1)} %bitcast.6) | data formatting | bytes 2359296
  190.9 0.0 copy-start.1
  190.9 0.0 copy-start
  190.9 4.9 %copy.16 = bf16[1,512,4608]{2,1,0:T(8,128)(2,1)} copy(bf16[1,512,4608]{2,1,0:T(8,128)(2,1)} %bitcast.5) | data formatting | bytes 9437184
  195.8 0.0 copy-done.1
  195.8 0.6 copy.17
  196.4 0.0 copy-done
  196.5 0.6 copy.18
Async XLA Ops:
  190.9 4.9 %copy-start.1 = (f32[18,1024]{1,0:T(8,128)S(1)}, f32[18,1024]{1,0:T(8,128)}, u32[]{:S(2)}) copy-start(f32[18,1024]{1,0:T(8,128)} %get-tuple-element.18) | copy-start | bytes 221188
  190.9 5.5 %copy-start = (f32[18,1024]{1,0:T(8,128)S(1)}, f32[18,1024]{1,0:T(8,128)}, u32[]{:S(2)}) copy-start(f32[18,1024]{1,0:T(8,128)} %get-tuple-element.19) | copy-start | bytes 221188

commit v2 on v1

--- a/solution.py
+++ b/solution.py
@@ -34,10 +34,10 @@
 
 def kernel(
     params, tokens, cot, gain, glob, mom, prev,
-    new_params, grad_tokens, new_global, new_momentum,
-    tok, cc, invb, gb, nst, nnt, wg, gs, gr, gk, zs, zr, up, cr, s2, yr, s8, lr, tot,
+    new_params, tok, new_global, new_momentum,
+    cc, invb, gb, nst, nnt, wg, gs, gr, gk, zs, zr, up, cr, s2, yr, s8, lr, tot,
     xs, xr, xo, po, pz, pzr, pa, pfull,
-    a_s, a_r, b_s, b_r, z_s, z_r, c_s, c_r, y_s, y_r, l_s, l_r, loc, outs,
+    a_s, a_r, b_s, b_r, z_s, z_r, c_s, c_r, y_s, y_r, l_s, l_r, loc,
 ):
     rep = lax.axis_index("replica")
     fs = lax.axis_index("fsdp")
@@ -71,11 +71,16 @@
         side = (1 - half) if b < 2 else half
         return pl.multiple_of(plane * (D // 2) + side * Q, 128)
 
+    def tile(b, j):
+        return pl.ds(pl.multiple_of(column(b) + j * 128, 128), 128)
+
     my_rows = pl.multiple_of(par * S, 64)
     its_rows = pl.multiple_of((1 - par) * S, 64)
 
     loads = [
-        pltpu.make_async_copy(tokens.at[:, pl.ds(column(b), Q)], tok.at[b], loc.at[b])
+        pltpu.make_async_copy(
+            tokens.at[:, pl.ds(column(b), Q)], tok.at[:, pl.ds(column(b), Q)], loc.at[b]
+        )
         for b in range(4)
     ]
     load_cot = pltpu.make_async_copy(cot, cc.at[pl.ds(0, T)], loc.at[4])
@@ -91,6 +96,8 @@
     load_w.start()
     pl.semaphore_wait(barrier, len(peers))
 
+    send_prev = remote(prev, po, c_s, c_r, 0, dev_c)
+    send_prev.start()
     send_cot = remote(cot, cc.at[pl.ds(T, T)], a_s, a_r, 0, dev_a)
     send_cot.start()
     send_w = remote(params, wg.at[1, pl.ds(my_rows, S)], b_s, b_r, 0, dev_b)
@@ -105,8 +112,25 @@
     ]
     for cp in far_w:
         cp.start()
-    send_prev = remote(prev, po, c_s, c_r, 0, dev_c)
-    send_prev.start()
+
+    send_prev.wait_recv()
+    wide = pl.ds(pl.multiple_of(core * (HV // 2), 128), HV // 2)
+    pz[...] = jnp.zeros_like(pz)
+
+    @pl.when(core == 0)
+    def _():
+        pz[0:OWN, :] = prev[:, wide]
+        pz[OWN : 2 * OWN, :] = po[:, wide]
+
+    @pl.when(core == 1)
+    def _():
+        pz[0:OWN, :] = po[:, wide]
+        pz[OWN : 2 * OWN, :] = prev[:, wide]
+
+    pzr[zl] = pz[...].astype(BF16)
+    prev_l = [remote(pzr.at[zl], pzr.at[zl], l_s, l_r, d, dev_l[d]) for d in range(3)]
+    for cp in prev_l:
+        cp.start()
 
     for b in range(4):
         gb[b] = gain[:, pl.ds(column(b), Q)]
@@ -119,7 +143,7 @@
         acc = jnp.zeros((32, 128), F32)
         for b in range(4):
             for j in range(Q // 128):
-                v = tok[b, rows, j * 128 : (j + 1) * 128].astype(F32)
+                v = tok[rows, tile(b, j)].astype(F32)
                 acc = acc + v * v
         inv = lax.rsqrt(jnp.sum(acc, axis=-1, keepdims=True) * (1.0 / D) + eps)
         invb[rows, :] = jnp.broadcast_to(inv, (32, 128))
@@ -128,7 +152,7 @@
         @pl.loop(0, Q // 128)
         def _(j):
             cols = pl.ds(pl.multiple_of(j * 128, 128), 128)
-            v = tok[b, :, cols].astype(F32) * invb[...] * gb[b, :, cols]
+            v = tok[:, tile(b, j)].astype(F32) * invb[...] * gb[b, :, cols]
             put(cols, v.T.astype(BF16))
 
     def put_send(o):
@@ -150,40 +174,26 @@
             cp.start()
             send_n.append(cp)
 
-    send_prev.wait_recv()
-    wide = pl.ds(pl.multiple_of(core * (HV // 2), 128), HV // 2)
-    pz[...] = jnp.zeros_like(pz)
-
-    @pl.when(core == 0)
-    def _():
-        pz[0:OWN, :] = prev[:, wide]
-        pz[OWN : 2 * OWN, :] = po[:, wide]
-
-    @pl.when(core == 1)
-    def _():
-        pz[0:OWN, :] = po[:, wide]
-        pz[OWN : 2 * OWN, :] = prev[:, wide]
-
-    pzr[zl] = pz[...].astype(BF16)
-    prev_l = [remote(pzr.at[zl], pzr.at[zl], l_s, l_r, d, dev_l[d]) for d in range(3)]
-    for cp in prev_l:
-        cp.start()
-
     for o in range(2):
         normed(2 + o, put_own(o))
 
-    for cp in prev_l:
-        cp.wait_recv()
-    for k in range(4):
-        pa[k * 36 : (k + 1) * 36, :] = pzr[k, 0:36, :].astype(F32)
     y_rows = pl.ds(pl.multiple_of(y * YR, 16), YR)
-    pfull[core, y_rows, :] = pa[...].astype(BF16)
-    prev_y = [
-        remote(pfull.at[core, y_rows], pfull.at[core, y_rows], y_s, y_r, d, dev_y[d])
-        for d in range(3)
-    ]
-    for cp in prev_y:
-        cp.start()
+    prev_y = []
+
+    def prev_to_y():
+        for cp in prev_l:
+            cp.wait_recv()
+        for k in range(4):
+            pa[k * 36 : (k + 1) * 36, :] = pzr[k, 0:36, :].astype(F32)
+        pfull[core, y_rows, :] = pa[...].astype(BF16)
+        prev_y.extend(
+            [
+                remote(pfull.at[core, y_rows], pfull.at[core, y_rows], y_s, y_r, d, dev_y[d])
+                for d in range(3)
+            ]
+        )
+        for cp in prev_y:
+            cp.start()
 
     forward = [
         remote(
@@ -228,45 +238,20 @@
         zs[c] = (gk[0, c] + gr[0, c].astype(F32)).astype(BF16)
         send_s(c).start()
 
-    pass_on(0)
-    for cp in prev_y:
-        cp.wait_recv()
-    prev_c = remote(pfull.at[core], pfull.at[core], c_s, c_r, 1, dev_c)
-    prev_c.start()
-    pass_on(1)
-    load_cot.wait()
-    load_w.wait()
-    send_cot.wait_recv()
-    give(0)
-    pass_on(2)
-    keep(0)
-    pass_on(3)
-    far_sum(0)
-    far_sum(1)
-    give(1)
-    far_sum(2)
-    far_sum(3)
-
-    send_w.wait_recv()
-    for cp in forward:
-        cp.wait_recv()
-
-    def dn(first, put):
-        for o in range(2):
-
-            @pl.loop(0, 3)
-            def _(n):
-                rows = pl.ds(pl.multiple_of(n * 384, 128), 384)
-                cols = pl.ds(pl.multiple_of(o * Q + n * 384, 128), 384)
-                put(
-                    cols,
-                    lax.dot_general(
-                        cc[first : first + T, :],
-                        wg[o, rows, :],
-                        (((1,), (1,)), ((), ())),
-                        preferred_element_type=F32,
-                    ),
-                )
+    def dn(o, first, put):
+        @pl.loop(0, 3)
+        def _(n):
+            rows = pl.ds(pl.multiple_of(n * 384, 128), 384)
+            cols = pl.ds(pl.multiple_of(o * Q + n * 384, 128), 384)
+            put(
+                cols,
+                lax.dot_general(
+                    cc[first : first + T, :],
+                    wg[o, rows, :],
+                    (((1,), (1,)), ((), ())),
+                    preferred_element_type=F32,
+                ),
+            )
 
     def put_xs(cols, v):
         xs[:, cols] = v.astype(BF16)
@@ -274,17 +259,12 @@
     def put_xo(cols, v):
         xo[:, cols] = v
 
-    dn(T, put_xs)
+    own_plane = pl.ds(Q, Q)
+    send_x1 = remote(xs.at[:, own_plane], xr.at[:, own_plane], a_s, a_r, 5 + NT, dev_a)
     send_x = []
     for t in range(NT):
-        rows = pl.ds(t * TR, TR)
-        cp = remote(xs.at[rows], xr.at[rows], a_s, a_r, 5 + t, dev_a)
-        cp.start()
-        send_x.append(cp)
-    keep(1)
-    dn(0, put_xo)
-
-    stores = []
+        at = (pl.ds(t * TR, TR), pl.ds(0, Q))
+        send_x.append(remote(xs.at[at], xr.at[at], a_s, a_r, 5 + t, dev_a))
 
     def finish(t):
         send_x[t].wait_recv()
@@ -296,7 +276,7 @@
 
             def parts(b, j):
                 cols = slice(j * 128, (j + 1) * 128)
-                unit = tok[b, rows, cols].astype(F32) * inv
+                unit = tok[rows, tile(b, j)].astype(F32) * inv
                 at = (b % 2) * Q + j * 128
                 if b < 2:
                     d = xr[rows, at : at + 128].astype(F32)
@@ -313,16 +293,7 @@
             for b in range(4):
                 for j in range(Q // 128):
                     unit, scaled = parts(b, j)
-                    tok[b, rows, j * 128 : (j + 1) * 128] = (inv * (scaled - unit * mean)).astype(BF16)
-
-        for b in range(4):
-            cp = pltpu.make_async_copy(
-                tok.at[b, pl.ds(t * TR, TR)],
-                grad_tokens.at[pl.ds(t * TR, TR), pl.ds(column(b), Q)],
-                outs.at[t, b],
-            )
-            cp.start()
-            stores.append(cp)
+                    tok[rows, tile(b, j)] = (inv * (scaled - unit * mean)).astype(BF16)
 
     def send_up(c):
         return remote(up.at[2 * c + 1 - core], cr.at[c], c_s, c_r, 2 + c, dev_c)
@@ -342,8 +313,6 @@
         return remote(tot.at[2 * c + core], tot.at[2 * c + core], c_s, c_r, 6 + c, dev_c)
 
     def update(c):
-        if c == 0:
-            prev_c.wait_recv()
         send_g(1, c).wait_recv()
         send_s(c).wait_recv()
         for k in range(2):
@@ -353,6 +322,8 @@
             now = (wg[1, pl.ds(my_rows, S), cols].astype(F32) - inner_rate * grad).astype(BF16)
             up[2 * c + k] = now
         send_up(c).start()
+
+    def mix(c):
         for k in range(2):
             cols = slice(c * CW + k * 128, c * CW + (k + 1) * 128)
             at = (c % 2) * CW + k * 128
@@ -380,29 +351,64 @@
         tot[2 * c + core] = s8[c, pl.ds(window(zl), WR), :] + lr[c, 0] + lr[c, 1] + lr[c, 2]
         send_tot(c).start()
 
+    pass_on(0)
+    pass_on(1)
+    load_cot.wait()
+    load_w.wait()
+    send_cot.wait_recv()
+    give(0)
+    send_w.wait_recv()
+    dn(1, T, put_xs)
+    send_x1.start()
+    pass_on(2)
+    keep(0)
+    far_sum(0)
+    far_sum(1)
+    pass_on(3)
+    far_sum(2)
+    give(1)
+    far_sum(3)
+    dn(1, 0, put_xo)
+    keep(1)
+    for cp in forward:
+        cp.wait_recv()
+    dn(0, T, put_xs)
+    for cp in send_x:
+        cp.start()
+    dn(0, 0, put_xo)
+
     update(0)
+    both_cores(0)
+    update(1)
+    all_y(0)
+    both_cores(1)
+    update(2)
+    all_y(1)
+    both_cores(2)
+    send_x1.wait_recv()
     finish(0)
-    both_cores(0)
+    all_y(2)
     finish(1)
-    all_y(0)
-    update(1)
     finish(2)
+    finish(3)
+    update(3)
+    finish(4)
+    both_cores(3)
+    prev_to_y()
+    finish(5)
+    all_y(3)
     all_l(0)
-    both_cores(1)
-    finish(3)
-    all_y(1)
-    update(2)
-    finish(4)
     all_l(1)
-    both_cores(2)
-    update(3)
-    finish(5)
-    all_y(2)
-    both_cores(3)
+    all_l(2)
+    for cp in prev_y:
+        cp.wait_recv()
+    prev_c = remote(pfull.at[core], pfull.at[core], c_s, c_r, 1, dev_c)
+    prev_c.start()
     finish(6)
-    all_l(2)
-    all_y(3)
     all_l(3)
+    prev_c.wait_recv()
+    for c in range(NC):
+        mix(c)
 
     for c in range(NC):
         send_tot(c).wait_recv()
@@ -420,7 +426,7 @@
         new_global[:, cols] = glob[:, cols] - outer_rate * (delta + nesterov * moved)
     finish(7)
 
-    for cp in [send_cot, send_w, send_prev, prev_c] + far_w + forward + send_n + send_x + prev_l + prev_y:
+    for cp in [send_cot, send_w, send_prev, prev_c, send_x1] + far_w + forward + send_n + send_x + prev_l + prev_y:
         cp.wait_send()
     for c in range(NC):
         send_g(0, c).wait_send()
@@ -431,8 +437,6 @@
         for d in range(3):
             send_y(c, d).wait_send()
             send_l(c, d).wait_send()
-    for cp in stores:
-        cp.wait()
 
 
 def shards(params, tokens, cotangent, gain, glob, momentum, prev_global):
@@ -442,15 +446,14 @@
     out = pl.pallas_call(
         kernel,
         out_shape=(
-            jax.ShapeDtypeStruct((S, HV), BF16),
-            jax.ShapeDtypeStruct((T, D), BF16),
-            jax.ShapeDtypeStruct((OWN, HV), F32),
-            jax.ShapeDtypeStruct((OWN, HV), F32),
+            pltpu.VMEM((S, HV), BF16),
+            pltpu.VMEM((T, D), BF16),
+            pltpu.VMEM((OWN, HV), F32),
+            pltpu.VMEM((OWN, HV), F32),
         ),
         in_specs=[hbm, hbm, hbm, vmem, vmem, vmem, vmem],
-        out_specs=(vmem, hbm, vmem, vmem),
+        out_specs=(vmem, vmem, vmem, vmem),
         scratch_shapes=[
-            pltpu.VMEM((4, T, Q), BF16),
             pltpu.VMEM((2 * T, HV), BF16),
             pltpu.VMEM((T, 128), F32),
             pltpu.VMEM((4, 1, Q), F32),
@@ -477,17 +480,16 @@
             pltpu.VMEM((4, PZ, HV // 2), BF16),
             pltpu.VMEM((YR, HV // 2), F32),
             pltpu.VMEM((2, S, HV // 2), BF16),
-            dma((5 + NT,)), dma((5 + NT,)),
+            dma((6 + NT,)), dma((6 + NT,)),
             dma((5 + 2 * NC,)), dma((5 + 2 * NC,)),
             dma((NZ + NC,)), dma((NZ + NC,)),
             dma((2 + 2 * NC,)), dma((2 + 2 * NC,)),
             dma((3 + 3 * NC,)), dma((3 + 3 * NC,)),
             dma((3 + 3 * NC,)), dma((3 + 3 * NC,)),
             dma((6,)),
-            dma((NT, 4)),
         ],
         compiler_params=pltpu.CompilerParams(
-            collective_id=0, has_side_effects=True, vmem_limit_bytes=60 * 1024 * 1024
+            collective_id=0, has_side_effects=True, vmem_limit_bytes=54 * 1024 * 1024
         ),
         cost_estimate=pl.CostEstimate(
             flops=4 * T * D * HV, bytes_accessed=16 * 1024 * 1024, transcendentals=T

time: 197 us -> 154 us (0.78)
  Pallas kernels: 187 us -> 148 us
  local copies, waits for them, and re-layouts: 9.86 us -> 5.83 us
    pallas_call x1, Pallas kernels: 187 us -> 148 us  [shards(): pl.pallas_call(kernel, out_shape=(pltpu.VMEM((S, HV), BF16), pltpu.VMEM((...]
    unnamed x8 -> x4, local copies, waits for them, and re-layouts: 8.52 us -> 4.48 us
where the time goes in v2:
time: 154 us
  Pallas kernels  148 us (96%)
  local copies, waits for them, and re-layouts  5.83 us (4%)
    pallas_call x1, Pallas kernels, shards(): pl.pallas_call(kernel, out_shape=(pltpu.VMEM((S, HV), BF16), pltpu.VMEM((...  148 us
    unnamed x4, local copies, waits for them, and re-layouts  4.48 us

profile of v2, /device:TPU:1, one launch (start us, length us, event | category | flops | bytes accessed | tf_op | source)
XLA Modules:
  0.0 154.2 jit_solution(13221095996175960158)
XLA Ops:
  0.6 1.3 reshape.11.gain
  2.0 147.7 %diloco.1 = (bf16[576,1024]{1,0:T(8,128)(2,1)S(1)}, bf16[512,4608]{1,0:T(8,128)(2,1)S(1)}, f32[18,1024]{1,0:T(8,128)S(1)}, f32[18,1024]{1,0:T(8,128)S(1)}) custom-call(bf16[576,1024]{1,0:T(8,128)(2,1)} %bitcast.8, bf16[512,4608]{1,0:T(8,128)(2,1)} %bitcast.7, bf16[512,1024]{1,0:T(8,128)(2,1)} %bitcast.9, f32[1,4608]{1,0:T(1,128)} %reshape.11.gain, ...), custom_call_target="tpu_custom_call" | custom-call | flops 9663676416 | bytes 16777216 | tf_op jit(solution)/shard_map/diloco/pallas_call | solution.py:446
  149.7 1.0 copy.15
  150.7 2.2 %copy.16 = bf16[1,512,4608]{2,1,0:T(8,128)(2,1)} copy(bf16[1,512,4608]{2,1,0:T(8,128)(2,1)S(1)} %bitcast.5) | data formatting | bytes 9437184
  152.9 0.6 copy.17
  153.6 0.6 copy.18

commit v3 on v2

--- a/solution.py
+++ b/solution.py
@@ -1,3 +1,5 @@
+import functools
+
 import jax
 import jax.numpy as jnp
 from jax import lax
@@ -35,8 +37,8 @@
 def kernel(
     params, tokens, cot, gain, glob, mom, prev,
     new_params, tok, new_global, new_momentum,
-    cc, invb, gb, nst, nnt, wg, gs, gr, gk, zs, zr, up, cr, s2, yr, s8, lr, tot,
-    xs, xr, xo, po, pz, pzr, pa, pfull,
+    cc, invb, gv, nst, nnt, wg, gs, gr, gk, zs, zr, up, cr, s2, yr, s8, lr, tot,
+    xs, xa, po, pz, pzr, pa, pfull,
     a_s, a_r, b_s, b_r, z_s, z_r, c_s, c_r, y_s, y_r, l_s, l_r, loc,
 ):
     rep = lax.axis_index("replica")
@@ -78,13 +80,11 @@
     its_rows = pl.multiple_of((1 - par) * S, 64)
 
     loads = [
-        pltpu.make_async_copy(
-            tokens.at[:, pl.ds(column(b), Q)], tok.at[:, pl.ds(column(b), Q)], loc.at[b]
-        )
-        for b in range(4)
+        pltpu.make_async_copy(tokens, tok, loc.at[0]),
+        pltpu.make_async_copy(gain, gv.at[0], loc.at[1]),
     ]
-    load_cot = pltpu.make_async_copy(cot, cc.at[pl.ds(0, T)], loc.at[4])
-    load_w = pltpu.make_async_copy(params, wg.at[1, pl.ds(my_rows, S)], loc.at[5])
+    load_cot = pltpu.make_async_copy(cot, cc.at[pl.ds(0, T)], loc.at[2])
+    load_w = pltpu.make_async_copy(params, wg.at[1, pl.ds(my_rows, S)], loc.at[3])
 
     barrier = pltpu.get_barrier_semaphore()
     peers = [dev_a, dev_b, dev_z, dev_c] + dev_y + dev_l
@@ -132,8 +132,6 @@
     for cp in prev_l:
         cp.start()
 
-    for b in range(4):
-        gb[b] = gain[:, pl.ds(column(b), Q)]
     for cp in loads:
         cp.wait()
 
@@ -141,19 +139,19 @@
     def _(i):
         rows = pl.ds(pl.multiple_of(i * 32, 32), 32)
         acc = jnp.zeros((32, 128), F32)
-        for b in range(4):
-            for j in range(Q // 128):
-                v = tok[rows, tile(b, j)].astype(F32)
-                acc = acc + v * v
+        for j in range(D // 128):
+            v = tok[rows, j * 128 : (j + 1) * 128].astype(F32)
+            acc = acc + v * v
         inv = lax.rsqrt(jnp.sum(acc, axis=-1, keepdims=True) * (1.0 / D) + eps)
         invb[rows, :] = jnp.broadcast_to(inv, (32, 128))
 
     def normed(b, put):
         @pl.loop(0, Q // 128)
         def _(j):
-            cols = pl.ds(pl.multiple_of(j * 128, 128), 128)
-            v = tok[:, tile(b, j)].astype(F32) * invb[...] * gb[b, :, cols]
-            put(cols, v.T.astype(BF16))
+            rows = pl.ds(pl.multiple_of(j * 128, 128), 128)
+            cols = tile(b, j)
+            v = tok[:, cols].astype(F32) * invb[...] * gv[:, cols]
+            put(rows, v.T.astype(BF16))
 
     def put_send(o):
         def put(rows, v):
@@ -242,9 +240,9 @@
         @pl.loop(0, 3)
         def _(n):
             rows = pl.ds(pl.multiple_of(n * 384, 128), 384)
-            cols = pl.ds(pl.multiple_of(o * Q + n * 384, 128), 384)
             put(
-                cols,
+                o,
+                n * 384,
                 lax.dot_general(
                     cc[first : first + T, :],
                     wg[o, rows, :],
@@ -253,18 +251,22 @@
                 ),
             )
 
-    def put_xs(cols, v):
-        xs[:, cols] = v.astype(BF16)
-
-    def put_xo(cols, v):
-        xo[:, cols] = v
+    def put_xs(o, at, v):
+        xs[:, pl.ds(pl.multiple_of(o * Q + at, 128), 384)] = v.astype(BF16)
+
+    def put_xo(o, at, v):
+        xa[:, pl.ds(pl.multiple_of(column(2 + o) + at, 128), 384)] = v.astype(BF16)
 
     own_plane = pl.ds(Q, Q)
-    send_x1 = remote(xs.at[:, own_plane], xr.at[:, own_plane], a_s, a_r, 5 + NT, dev_a)
+    send_x1 = remote(
+        xs.at[:, own_plane], xa.at[:, pl.ds(column(3), Q)], a_s, a_r, 5 + NT, dev_a
+    )
     send_x = []
     for t in range(NT):
-        at = (pl.ds(t * TR, TR), pl.ds(0, Q))
-        send_x.append(remote(xs.at[at], xr.at[at], a_s, a_r, 5 + t, dev_a))
+        rows = pl.ds(t * TR, TR)
+        send_x.append(
+            remote(xs.at[rows, pl.ds(0, Q)], xa.at[rows, pl.ds(column(2), Q)], a_s, a_r, 5 + t, dev_a)
+        )
 
     def finish(t):
         send_x[t].wait_recv()
@@ -274,26 +276,19 @@
             rows = pl.ds(pl.multiple_of(t * TR + i * 16, 16), 16)
             inv = invb[rows, :]
 
-            def parts(b, j):
+            def parts(j):
                 cols = slice(j * 128, (j + 1) * 128)
-                unit = tok[rows, tile(b, j)].astype(F32) * inv
-                at = (b % 2) * Q + j * 128
-                if b < 2:
-                    d = xr[rows, at : at + 128].astype(F32)
-                else:
-                    d = xo[rows, at : at + 128]
-                return unit, gb[b, :, cols] * d
+                unit = tok[rows, cols].astype(F32) * inv
+                return unit, gv[:, cols] * xa[rows, cols].astype(F32)
 
             acc = jnp.zeros((16, 128), F32)
-            for b in range(4):
-                for j in range(Q // 128):
-                    unit, scaled = parts(b, j)
-                    acc = acc + unit * scaled
+            for j in range(D // 128):
+                unit, scaled = parts(j)
+                acc = acc + unit * scaled
             mean = jnp.sum(acc, axis=-1, keepdims=True) * (1.0 / D)
-            for b in range(4):
-                for j in range(Q // 128):
-                    unit, scaled = parts(b, j)
-                    tok[rows, tile(b, j)] = (inv * (scaled - unit * mean)).astype(BF16)
+            for j in range(D // 128):
+                unit, scaled = parts(j)
+                tok[rows, j * 128 : (j + 1) * 128] = (inv * (scaled - unit * mean)).astype(BF16)
 
     def send_up(c):
         return remote(up.at[2 * c + 1 - core], cr.at[c], c_s, c_r, 2 + c, dev_c)
@@ -389,26 +384,25 @@
     finish(0)
     all_y(2)
     finish(1)
+    update(3)
     finish(2)
-    finish(3)
-    update(3)
-    finish(4)
     both_cores(3)
     prev_to_y()
-    finish(5)
+    finish(3)
     all_y(3)
-    all_l(0)
-    all_l(1)
-    all_l(2)
     for cp in prev_y:
         cp.wait_recv()
     prev_c = remote(pfull.at[core], pfull.at[core], c_s, c_r, 1, dev_c)
     prev_c.start()
-    finish(6)
+    all_l(0)
+    all_l(1)
+    all_l(2)
+    finish(4)
     all_l(3)
     prev_c.wait_recv()
     for c in range(NC):
         mix(c)
+    finish(5)
 
     for c in range(NC):
         send_tot(c).wait_recv()
@@ -424,6 +418,7 @@
         moved = nesterov * mom[:, cols] + delta
         new_momentum[:, cols] = moved
         new_global[:, cols] = glob[:, cols] - outer_rate * (delta + nesterov * moved)
+    finish(6)
     finish(7)
 
     for cp in [send_cot, send_w, send_prev, prev_c, send_x1] + far_w + forward + send_n + send_x + prev_l + prev_y:
@@ -437,6 +432,15 @@
         for d in range(3):
             send_y(c, d).wait_send()
             send_l(c, d).wait_send()
+
+
+def store(n, *refs):
+    sems = refs[-1]
+    copies = [pltpu.make_async_copy(refs[i], refs[n + i], sems.at[i]) for i in range(n)]
+    for cp in copies:
+        cp.start()
+    for cp in copies:
+        cp.wait()
 
 
 def shards(params, tokens, cotangent, gain, glob, momentum, prev_global):
@@ -451,12 +455,12 @@
             pltpu.VMEM((OWN, HV), F32),
             pltpu.VMEM((OWN, HV), F32),
         ),
-        in_specs=[hbm, hbm, hbm, vmem, vmem, vmem, vmem],
+        in_specs=[hbm, hbm, hbm, hbm, vmem, vmem, vmem],
         out_specs=(vmem, vmem, vmem, vmem),
         scratch_shapes=[
             pltpu.VMEM((2 * T, HV), BF16),
             pltpu.VMEM((T, 128), F32),
-            pltpu.VMEM((4, 1, Q), F32),
+            pltpu.VMEM((1, D), F32),
             pltpu.VMEM((2, Q, T), BF16),
             pltpu.VMEM((2, Q, 2 * T), BF16),
             pltpu.VMEM((2, Q, HV), BF16),
@@ -473,8 +477,7 @@
             pltpu.VMEM((NC, 3, WR, 128), F32),
             pltpu.VMEM((2 * NC, WR, 128), F32),
             pltpu.VMEM((T, 2 * Q), BF16),
-            pltpu.VMEM((T, 2 * Q), BF16),
-            pltpu.VMEM((T, 2 * Q), F32),
+            pltpu.VMEM((T, D), BF16),
             pltpu.VMEM((OWN, HV), F32),
             pltpu.VMEM((PZ, HV // 2), F32),
             pltpu.VMEM((4, PZ, HV // 2), BF16),
@@ -486,7 +489,7 @@
             dma((2 + 2 * NC,)), dma((2 + 2 * NC,)),
             dma((3 + 3 * NC,)), dma((3 + 3 * NC,)),
             dma((3 + 3 * NC,)), dma((3 + 3 * NC,)),
-            dma((6,)),
+            dma((4,)),
         ],
         compiler_params=pltpu.CompilerParams(
             collective_id=0, has_side_effects=True, vmem_limit_bytes=54 * 1024 * 1024
@@ -495,7 +498,16 @@
             flops=4 * T * D * HV, bytes_accessed=16 * 1024 * 1024, transcendentals=T
         ),
         name="diloco",
-    )(params[0], tokens[0], cotangent[0], gain.reshape(1, D), glob, momentum, prev_global)
+    )(params[0], tokens[0], cotangent[0], gain, glob, momentum, prev_global)
+    out = pl.pallas_call(
+        functools.partial(store, len(out)),
+        out_shape=tuple(jax.ShapeDtypeStruct(v.shape, v.dtype) for v in out),
+        in_specs=[vmem] * len(out),
+        out_specs=[hbm] * len(out),
+        scratch_shapes=[dma((len(out),))],
+        compiler_params=pltpu.CompilerParams(vmem_limit_bytes=1024 * 1024),
+        name="store",
+    )(*out)
     return (out[0][None], out[1][None], out[2], out[3])
 
 

time: 154 us -> 144 us (0.935)
  local copies, waits for them, and re-layouts: 5.83 us -> 0 us
  Pallas kernels: 148 us -> 143 us
    pallas_call x1, Pallas kernels: 148 us -> 140 us  [shards(): pl.pallas_call(kernel, out_shape=(pltpu.VMEM((S, HV), BF16), pltpu.VMEM((...]
    unnamed x4 -> x0, local copies, waits for them, and re-layouts: 4.48 us -> none
    pallas_call x0 -> x1, Pallas kernels: none -> 2.65 us  [shards(): pl.pallas_call(functools.partial(store, len(out)), out_shape=tuple((jax.S...]
where the time goes in v3:
time: 144 us
  Pallas kernels  143 us (99%)
    pallas_call x1, Pallas kernels, shards(): pl.pallas_call(kernel, out_shape=(pltpu.VMEM((S, HV), BF16), pltpu.VMEM((...  140 us

profile of v3, /device:TPU:1, one launch (start us, length us, event | category | flops | bytes accessed | tf_op | source)
XLA Modules:
  0.0 143.8 jit_solution(9270904364303861506)
XLA Ops:
  0.6 140.5 %diloco.1 = (bf16[576,1024]{1,0:T(8,128)(2,1)S(1)}, bf16[512,4608]{1,0:T(8,128)(2,1)S(1)}, f32[18,1024]{1,0:T(8,128)S(1)}, f32[18,1024]{1,0:T(8,128)S(1)}) custom-call(bf16[576,1024]{1,0:T(8,128)(2,1)} %bitcast.7, bf16[512,4608]{1,0:T(8,128)(2,1)} %bitcast.5, bf16[512,1024]{1,0:T(8,128)(2,1)} %bitcast.9, f32[4608]{0:T(1024)} %gain.1, f32[18,1024]{1,0:T(8,128)} %glob.1, ...), custom_call_target="tpu_custom_call" | custom-call | flops 9663676416 | bytes 16777216 | tf_op jit(solution)/shard_map/diloco/pallas_call | solution.py:450
  141.1 2.6 %store.1 = (bf16[576,1024]{1,0:T(8,128)(2,1)}, bf16[512,4608]{1,0:T(8,128)(2,1)}, f32[18,1024]{1,0:T(8,128)}, f32[18,1024]{1,0:T(8,128)}) custom-call(bf16[576,1024]{1,0:T(8,128)(2,1)S(1)} %get-tuple-element.12.refs_0_, bf16[512,4608]{1,0:T(8,128)(2,1)S(1)} %get-tuple-element.13.refs_1_, f32[18,1024]{1,0:T(8,128)S(1)} %get-tuple-element.14.refs_2_, ...), custom_call_target="tpu_custom_call" | custom-call | tf_op jit(solution)/shard_map/store/pallas_call | solution.py:502

commit v4 on v3

--- a/solution.py
+++ b/solution.py
@@ -1,5 +1,3 @@
-import functools
-
 import jax
 import jax.numpy as jnp
 from jax import lax
@@ -29,15 +27,24 @@
 NZ = 4
 ZR = S // NZ
 YR = S // 4
-WR = 40
+WR = 24
 OWN = 18
 PZ = 48
+
+
+def pieces(core):
+    out = []
+    for plane in (0, D // 2):
+        out.append((plane, pl.multiple_of(plane + core * Q, 128), 512))
+        out.append((plane + 512, pl.multiple_of(plane + (1 - core) * 512, 128), Q))
+        out.append((plane + 512 + Q, plane + 512 + Q, Q - 512))
+    return out
 
 
 def kernel(
     params, tokens, cot, gain, glob, mom, prev,
     new_params, tok, new_global, new_momentum,
-    cc, invb, gv, nst, nnt, wg, gs, gr, gk, zs, zr, up, cr, s2, yr, s8, lr, tot,
+    cc, invb, gn, gv, nst, nnt, wg, gs, gr, gk, zs, zr, up, yr, s8, lr, tot,
     xs, xa, po, pz, pzr, pa, pfull,
     a_s, a_r, b_s, b_r, z_s, z_r, c_s, c_r, y_s, y_r, l_s, l_r, loc,
 ):
@@ -48,15 +55,23 @@
     y = lax.div(rep, 8)
     x = lax.rem(fs, 4)
     zh = lax.div(fs, 4)
-    half = lax.div(x, 2)
-    par = lax.rem(x, 2)
-
-    dev_a = (rep, zh * 4 + lax.rem(jnp.where(par == 0, x + 3, x + 1), 4))
-    dev_b = (rep, zh * 4 + half * 2 + (1 - par))
+    half = jnp.where(core == 0, lax.div(x, 2), 1 - lax.rem(lax.div(x + 1, 2), 2))
+    par = jnp.where(core == 0, lax.rem(x, 2), lax.div(x, 2))
+    beside = x + 1 - 2 * lax.rem(x, 2)
+
+    dev_a = (rep, zh * 4 + jnp.where(core == 0, 3 - x, beside))
+    dev_b = (rep, zh * 4 + jnp.where(core == 0, beside, 3 - x))
     dev_z = (rep, (1 - zh) * 4 + x)
     dev_c = ((y * 4 + zl) * 2 + (1 - core), fs)
-    dev_y = [((lax.rem(y + d, 4) * 4 + zl) * 2 + core, fs) for d in (1, 2, 3)]
-    dev_l = [((y * 4 + lax.rem(zl + d, 4)) * 2 + core, fs) for d in (1, 2, 3)]
+
+    def dev_y(i):
+        return ((lax.rem(y + i // 2, 4) * 4 + zl) * 2 + lax.rem(core + i % 2, 2), fs)
+
+    def dev_l(i):
+        return ((y * 4 + lax.rem(zl + i // 2, 4)) * 2 + lax.rem(core + i % 2, 2), fs)
+
+    def dev_zl(pos):
+        return ((y * 4 + pos) * 2 + core, fs)
 
     def remote(src, dst, sends, recvs, i, dev):
         return pltpu.make_async_remote_copy(
@@ -78,16 +93,29 @@
 
     my_rows = pl.multiple_of(par * S, 64)
     its_rows = pl.multiple_of((1 - par) * S, 64)
+    base = jnp.where((core == 1) & (half == 0), 64, 0)
+    w_rows = pl.multiple_of(base + par * S, 64)
+
+    def w_part(k):
+        return pl.ds(pl.multiple_of(w_rows + k * ZR, 16), ZR)
+
+    first_lanes = (lax.broadcasted_iota(jnp.int32, (16, 128), 1) < 64) & (core == 1)
+
+    def exchange(v, u, mask):
+        return jnp.where(mask, u, v), jnp.where(mask, v, u)
 
     loads = [
-        pltpu.make_async_copy(tokens, tok, loc.at[0]),
-        pltpu.make_async_copy(gain, gv.at[0], loc.at[1]),
+        pltpu.make_async_copy(
+            tokens.at[:, pl.ds(start, width)], tok.at[:, pl.ds(place, width)], loc.at[4 + i]
+        )
+        for i, (start, place, width) in enumerate(pieces(core))
     ]
+    loads.append(pltpu.make_async_copy(gain, gn.at[0], loc.at[1]))
     load_cot = pltpu.make_async_copy(cot, cc.at[pl.ds(0, T)], loc.at[2])
-    load_w = pltpu.make_async_copy(params, wg.at[1, pl.ds(my_rows, S)], loc.at[3])
+    load_w = pltpu.make_async_copy(params, wg.at[1, pl.ds(w_rows, S)], loc.at[3])
 
     barrier = pltpu.get_barrier_semaphore()
-    peers = [dev_a, dev_b, dev_z, dev_c] + dev_y + dev_l
+    peers = [dev_a, dev_b, dev_z] + [dev_y(i) for i in range(1, 8)] + [dev_l(i) for i in range(2, 8)]
     for dev in peers:
         pl.semaphore_signal(barrier, inc=1, device_id=dev, device_id_type=MESH)
     for cp in loads:
@@ -100,18 +128,17 @@
     send_prev.start()
     send_cot = remote(cot, cc.at[pl.ds(T, T)], a_s, a_r, 0, dev_a)
     send_cot.start()
-    send_w = remote(params, wg.at[1, pl.ds(my_rows, S)], b_s, b_r, 0, dev_b)
+    send_w = remote(params, wg.at[1, pl.ds(w_rows, S)], b_s, b_r, 0, dev_b)
     send_w.start()
     far_w = [
         remote(
             params.at[pl.ds(k * ZR, ZR)],
-            wg.at[0, pl.ds(pl.multiple_of(my_rows + k * ZR, 16), ZR)],
+            wg.at[0, w_part(k)],
             z_s, z_r, k, dev_z,
         )
         for k in range(NZ)
     ]
-    for cp in far_w:
-        cp.start()
+    far_w[0].start()
 
     send_prev.wait_recv()
     wide = pl.ds(pl.multiple_of(core * (HV // 2), 128), HV // 2)
@@ -127,13 +154,53 @@
         pz[0:OWN, :] = po[:, wide]
         pz[OWN : 2 * OWN, :] = prev[:, wide]
 
-    pzr[zl] = pz[...].astype(BF16)
-    prev_l = [remote(pzr.at[zl], pzr.at[zl], l_s, l_r, d, dev_l[d]) for d in range(3)]
-    for cp in prev_l:
+    pair, place_in = lax.div(zl, 2), lax.rem(zl, 2)
+    edge = pair == place_in
+    pzr[pair, place_in] = pz[...].astype(BF16)
+    prev_l = remote(
+        pzr.at[pair, place_in], pzr.at[pair, place_in], l_s, l_r, 0, dev_zl(zl + 1 - 2 * place_in)
+    )
+    prev_l.start()
+    for cp in far_w[1:]:
         cp.start()
+
+    relay = [
+        pltpu.make_async_remote_copy(
+            src_ref=pzr.at[pair],
+            dst_ref=pzr.at[pair],
+            send_sem=l_s.at[1 + k],
+            recv_sem=l_r.at[1],
+            device_id=dev_zl((1 - pair) * 2 + k),
+            device_id_type=MESH,
+        )
+        for k in range(2)
+    ]
+
+    def pass_prev():
+        prev_l.wait_recv()
+
+        @pl.when(edge)
+        def _():
+            for cp in relay:
+                cp.start()
 
     for cp in loads:
         cp.wait()
+    for start, place, width in pieces(core):
+        gv[:, pl.ds(place, width)] = gn[:, start : start + width]
+    for plane in (0, D // 2):
+        at, to = slice(plane, plane + 128), slice(plane + 512 + Q, plane + 640 + Q)
+        gv[:, at], gv[:, to] = exchange(gv[:, at], gv[:, to], first_lanes[0:1, :])
+
+        @pl.when(core == 1)
+        def _():
+            @pl.loop(0, T // 16)
+            def _(i):
+                rows = pl.ds(pl.multiple_of(i * 16, 16), 16)
+                v, u = exchange(tok[rows, at].astype(F32), tok[rows, to].astype(F32), first_lanes)
+                tok[rows, at] = v.astype(BF16)
+                tok[rows, to] = u.astype(BF16)
+
 
     @pl.loop(0, T // 32)
     def _(i):
@@ -148,10 +215,13 @@
     def normed(b, put):
         @pl.loop(0, Q // 128)
         def _(j):
-            rows = pl.ds(pl.multiple_of(j * 128, 128), 128)
             cols = tile(b, j)
-            v = tok[:, cols].astype(F32) * invb[...] * gv[:, cols]
-            put(rows, v.T.astype(BF16))
+            v = (tok[:, cols].astype(F32) * invb[...] * gv[:, cols]).T.astype(BF16)
+            side = (1 - half) if b < 2 else half
+            shift = jnp.where((core == 1) & (side == 0), 64, 0)
+            for k in range(2):
+                row = lax.rem(j * 128 + k * 64 - shift + Q, Q)
+                put(pl.ds(pl.multiple_of(row, 64), 64), v[k * 64 : (k + 1) * 64])
 
     def put_send(o):
         def put(rows, v):
@@ -166,8 +236,8 @@
     send_n = []
     for o in range(2):
         normed(o, put_send(o))
-        for p, start in enumerate((my_rows, its_rows)):
-            rows = pl.ds(start, S)
+        for p in range(2):
+            rows = pl.ds(pl.multiple_of(jnp.where(core == p, my_rows, its_rows), 64), S)
             cp = remote(nst.at[o, rows], nnt.at[o, rows, pl.ds(T, T)], a_s, a_r, 1 + 2 * o + p, dev_a)
             cp.start()
             send_n.append(cp)
@@ -179,14 +249,13 @@
     prev_y = []
 
     def prev_to_y():
-        for cp in prev_l:
-            cp.wait_recv()
+        relay[0].wait_recv()
         for k in range(4):
-            pa[k * 36 : (k + 1) * 36, :] = pzr[k, 0:36, :].astype(F32)
+            pa[k * 36 : (k + 1) * 36, :] = pzr[k // 2, k % 2, 0:36, :].astype(F32)
         pfull[core, y_rows, :] = pa[...].astype(BF16)
         prev_y.extend(
             [
-                remote(pfull.at[core, y_rows], pfull.at[core, y_rows], y_s, y_r, d, dev_y[d])
+                remote(pfull.at[core, y_rows], pfull.at[core, y_rows], y_s, y_r, d, dev_y(2 * d + 2))
                 for d in range(3)
             ]
         )
@@ -195,8 +264,8 @@
 
     forward = [
         remote(
-            wg.at[0, pl.ds(pl.multiple_of(my_rows + k * ZR, 16), ZR)],
-            wg.at[0, pl.ds(pl.multiple_of(my_rows + k * ZR, 16), ZR)],
+            wg.at[0, w_part(k)],
+            wg.at[0, w_part(k)],
             b_s, b_r, 1 + k, dev_b,
         )
         for k in range(NZ)
@@ -235,6 +304,11 @@
         send_g(0, c).wait_recv()
         zs[c] = (gk[0, c] + gr[0, c].astype(F32)).astype(BF16)
         send_s(c).start()
+
+    def wrap(o):
+        @pl.when(base == 64)
+        def _():
+            wg[o, 0:64, :] = wg[o, Q : Q + 64, :]
 
     def dn(o, first, put):
         @pl.loop(0, 3)
@@ -286,26 +360,34 @@
                 unit, scaled = parts(j)
                 acc = acc + unit * scaled
             mean = jnp.sum(acc, axis=-1, keepdims=True) * (1.0 / D)
-            for j in range(D // 128):
+
+            def result(j):
                 unit, scaled = parts(j)
-                tok[rows, j * 128 : (j + 1) * 128] = (inv * (scaled - unit * mean)).astype(BF16)
-
-    def send_up(c):
-        return remote(up.at[2 * c + 1 - core], cr.at[c], c_s, c_r, 2 + c, dev_c)
-
-    def send_y(c, d):
-        rows = pl.ds(pl.multiple_of(lax.rem(y + d + 1, 4) * YR, 16), YR)
-        return remote(s2.at[c, rows], yr.at[c, d], y_s, y_r, 3 + 3 * c + d, dev_y[d])
+                return inv * (scaled - unit * mean)
+
+            def put(j, v):
+                tok[rows, j * 128 : (j + 1) * 128] = v.astype(BF16)
+
+            for plane in (0, D // 256):
+                last = plane + (512 + Q) // 128
+                v, u = exchange(result(plane), result(last), first_lanes)
+                put(plane, v)
+                put(last, u)
+                for j in range(plane + 1, plane + D // 256):
+                    if j != last:
+                        put(j, result(j))
+
+    def send_y(c, i):
+        rows = pl.ds(pl.multiple_of(lax.rem(y + i // 2, 4) * YR, 16), YR)
+        src = up.at[2 * c + lax.rem(core + i % 2, 2), rows]
+        return remote(src, yr.at[c, i], y_s, y_r, 2 + 7 * c + i, dev_y(i))
 
     def window(pos):
-        return pl.multiple_of(pos * 36 - lax.rem(pos, 2) * 4, 8)
-
-    def send_l(c, d):
-        rows = pl.ds(window(lax.rem(zl + d + 1, 4)), WR)
-        return remote(s8.at[c, rows], lr.at[c, d], l_s, l_r, 3 + 3 * c + d, dev_l[d])
-
-    def send_tot(c):
-        return remote(tot.at[2 * c + core], tot.at[2 * c + core], c_s, c_r, 6 + c, dev_c)
+        return pl.ds(pl.multiple_of(lax.div(pos * OWN, 8) * 8, 8), WR)
+
+    def send_l(c, i):
+        pos = lax.rem(zl + i // 2, 4) * 2 + lax.rem(core + i % 2, 2)
+        return remote(s8.at[c, window(pos)], lr.at[c, i], l_s, l_r, 2 + 7 * c + i, dev_l(i))
 
     def update(c):
         send_g(1, c).wait_recv()
@@ -314,9 +396,10 @@
             part = slice(k * 128, (k + 1) * 128)
             cols = slice(c * CW + k * 128, c * CW + (k + 1) * 128)
             grad = gk[1, c, :, part] + gr[1, c, :, part].astype(F32) + zr[c, :, part].astype(F32)
-            now = (wg[1, pl.ds(my_rows, S), cols].astype(F32) - inner_rate * grad).astype(BF16)
+            now = (wg[1, pl.ds(w_rows, S), cols].astype(F32) - inner_rate * grad).astype(BF16)
             up[2 * c + k] = now
-        send_up(c).start()
+        for i in range(1, 8):
+            send_y(c, i).start()
 
     def mix(c):
         for k in range(2):
@@ -327,32 +410,31 @@
                 (1.0 - mix_weight) * up[2 * c + k].astype(F32) + mix_weight * old
             ).astype(BF16)
 
-    def both_cores(c):
-        send_up(c).wait_recv()
-        s2[c] = up[2 * c + core].astype(F32) + cr[c].astype(F32)
-        for d in range(3):
-            send_y(c, d).start()
-
     def all_y(c):
-        for d in range(3):
-            send_y(c, d).wait_recv()
-        s8[c] = s2[c, y_rows, :] + yr[c, 0] + yr[c, 1] + yr[c, 2]
-        for d in range(3):
-            send_l(c, d).start()
+        for i in range(1, 8):
+            send_y(c, i).wait_recv()
+        total = up[2 * c + core, y_rows, :].astype(F32)
+        for i in range(1, 8):
+            total = total + yr[c, i].astype(F32)
+        s8[c] = total
+        for i in range(1, 8):
+            send_l(c, i).start()
 
     def all_l(c):
-        for d in range(3):
-            send_l(c, d).wait_recv()
-        tot[2 * c + core] = s8[c, pl.ds(window(zl), WR), :] + lr[c, 0] + lr[c, 1] + lr[c, 2]
-        send_tot(c).start()
+        for i in range(1, 8):
+            send_l(c, i).wait_recv()
+        tot[2 * c + core] = s8[c, window(zl * 2 + core), :] + lr[c, 2] + lr[c, 4] + lr[c, 6]
+        tot[2 * c + 1 - core] = lr[c, 1] + lr[c, 3] + lr[c, 5] + lr[c, 7]
 
     pass_on(0)
     pass_on(1)
+    pass_prev()
     load_cot.wait()
     load_w.wait()
     send_cot.wait_recv()
     give(0)
     send_w.wait_recv()
+    wrap(1)
     dn(1, T, put_xs)
     send_x1.start()
     pass_on(2)
@@ -367,76 +449,85 @@
     keep(1)
     for cp in forward:
         cp.wait_recv()
+    wrap(0)
     dn(0, T, put_xs)
     for cp in send_x:
         cp.start()
     dn(0, 0, put_xo)
 
     update(0)
-    both_cores(0)
+    prev_to_y()
     update(1)
-    all_y(0)
-    both_cores(1)
-    update(2)
-    all_y(1)
-    both_cores(2)
-    send_x1.wait_recv()
-    finish(0)
-    all_y(2)
-    finish(1)
-    update(3)
-    finish(2)
-    both_cores(3)
-    prev_to_y()
-    finish(3)
-    all_y(3)
     for cp in prev_y:
         cp.wait_recv()
     prev_c = remote(pfull.at[core], pfull.at[core], c_s, c_r, 1, dev_c)
     prev_c.start()
+    all_y(0)
+    update(2)
+    prev_c.wait_recv()
+    mix(0)
+    mix(1)
+    all_y(1)
+    send_x1.wait_recv()
+    finish(0)
+    mix(2)
+    all_y(2)
+    finish(1)
+    update(3)
+    mix(3)
+    finish(2)
+    finish(3)
+    finish(4)
+    all_y(3)
     all_l(0)
     all_l(1)
     all_l(2)
-    finish(4)
+    finish(5)
+    finish(6)
     all_l(3)
-    prev_c.wait_recv()
-    for c in range(NC):
-        mix(c)
-    finish(5)
-
-    for c in range(NC):
-        send_tot(c).wait_recv()
+
     place = lax.rem(zl, 2) * 2 + core
     for j in range(HV // 128):
         cols = slice(j * 128, (j + 1) * 128)
         total = jnp.where(
             place < 2,
-            jnp.where(place == 0, tot[j, 0:18, :], tot[j, 18:36, :]),
-            jnp.where(place == 2, tot[j, 4:22, :], tot[j, 22:40, :]),
+            jnp.where(place == 0, tot[j, 0:18, :], tot[j, 2:20, :]),
+            jnp.where(place == 2, tot[j, 4:22, :], tot[j, 6:24, :]),
         )
         delta = glob[:, cols] - total * (1.0 / 32)
         moved = nesterov * mom[:, cols] + delta
         new_momentum[:, cols] = moved
         new_global[:, cols] = glob[:, cols] - outer_rate * (delta + nesterov * moved)
-    finish(6)
     finish(7)
 
-    for cp in [send_cot, send_w, send_prev, prev_c, send_x1] + far_w + forward + send_n + send_x + prev_l + prev_y:
+    for cp in [send_cot, send_w, send_prev, prev_c, send_x1, prev_l] + far_w + forward + send_n + send_x + prev_y:
         cp.wait_send()
+
+    @pl.when(edge)
+    def _():
+        for cp in relay:
+            cp.wait_send()
+
     for c in range(NC):
         send_g(0, c).wait_send()
         send_g(1, c).wait_send()
         send_s(c).wait_send()
-        send_up(c).wait_send()
-        send_tot(c).wait_send()
-        for d in range(3):
-            send_y(c, d).wait_send()
-            send_l(c, d).wait_send()
-
-
-def store(n, *refs):
-    sems = refs[-1]
-    copies = [pltpu.make_async_copy(refs[i], refs[n + i], sems.at[i]) for i in range(n)]
+        for i in range(1, 8):
+            send_y(c, i).wait_send()
+            send_l(c, i).wait_send()
+
+
+def store(params, tok, glob, mom, params_out, tokens_out, glob_out, mom_out, sems):
+    core = lax.rem(lax.axis_index("replica"), 2)
+    copies = [
+        pltpu.make_async_copy(
+            tok.at[:, pl.ds(place, width)], tokens_out.at[:, pl.ds(start, width)], sems.at[i]
+        )
+        for i, (start, place, width) in enumerate(pieces(core))
+    ]
+    n = len(copies)
+    for i, (src, dst) in enumerate(((params, params_out), (glob, glob_out), (mom, mom_out))):
+        copies.append(pltpu.make_async_copy(src, dst, sems.at[n + i]))
     for cp in copies:
         cp.start()
     for cp in copies:
@@ -461,35 +552,34 @@
             pltpu.VMEM((2 * T, HV), BF16),
             pltpu.VMEM((T, 128), F32),
             pltpu.VMEM((1, D), F32),
+            pltpu.VMEM((1, D), F32),
             pltpu.VMEM((2, Q, T), BF16),
             pltpu.VMEM((2, Q, 2 * T), BF16),
-            pltpu.VMEM((2, Q, HV), BF16),
+            pltpu.VMEM((2, Q + 64, HV), BF16),
             pltpu.VMEM((2, NC, S, CW), BF16),
             pltpu.VMEM((2, NC, S, CW), BF16),
             pltpu.VMEM((2, NC, S, CW), F32),
             pltpu.VMEM((NC, S, CW), BF16),
             pltpu.VMEM((NC, S, CW), BF16),
             pltpu.VMEM((2 * NC, S, 128), BF16),
-            pltpu.VMEM((NC, S, 128), BF16),
-            pltpu.VMEM((NC, S, 128), F32),
-            pltpu.VMEM((NC, 3, YR, 128), F32),
+            pltpu.VMEM((NC, 8, YR, 128), BF16),
             pltpu.VMEM((NC, YR, 128), F32),
-            pltpu.VMEM((NC, 3, WR, 128), F32),
+            pltpu.VMEM((NC, 8, WR, 128), F32),
             pltpu.VMEM((2 * NC, WR, 128), F32),
             pltpu.VMEM((T, 2 * Q), BF16),
             pltpu.VMEM((T, D), BF16),
             pltpu.VMEM((OWN, HV), F32),
             pltpu.VMEM((PZ, HV // 2), F32),
-            pltpu.VMEM((4, PZ, HV // 2), BF16),
+            pltpu.VMEM((2, 2, PZ, HV // 2), BF16),
             pltpu.VMEM((YR, HV // 2), F32),
             pltpu.VMEM((2, S, HV // 2), BF16),
             dma((6 + NT,)), dma((6 + NT,)),
             dma((5 + 2 * NC,)), dma((5 + 2 * NC,)),
             dma((NZ + NC,)), dma((NZ + NC,)),
-            dma((2 + 2 * NC,)), dma((2 + 2 * NC,)),
-            dma((3 + 3 * NC,)), dma((3 + 3 * NC,)),
-            dma((3 + 3 * NC,)), dma((3 + 3 * NC,)),
-            dma((4,)),
+            dma((2,)), dma((2,)),
+            dma((3 + 7 * NC,)), dma((3 + 7 * NC,)),
+            dma((3 + 7 * NC,)), dma((3 + 7 * NC,)),
+            dma((10,)),
         ],
         compiler_params=pltpu.CompilerParams(
             collective_id=0, has_side_effects=True, vmem_limit_bytes=54 * 1024 * 1024
@@ -500,11 +590,11 @@
         name="diloco",
     )(params[0], tokens[0], cotangent[0], gain, glob, momentum, prev_global)
     out = pl.pallas_call(
-        functools.partial(store, len(out)),
+        store,
         out_shape=tuple(jax.ShapeDtypeStruct(v.shape, v.dtype) for v in out),
         in_specs=[vmem] * len(out),
         out_specs=[hbm] * len(out),
-        scratch_shapes=[dma((len(out),))],
+        scratch_shapes=[dma((9,))],
         compiler_params=pltpu.CompilerParams(vmem_limit_bytes=1024 * 1024),
         name="store",
     )(*out)

time: 144 us -> 137 us (0.951)
  Pallas kernels: 143 us -> 136 us
    pallas_call x1, Pallas kernels: 140 us -> 133 us  [shards(): pl.pallas_call(kernel, out_shape=(pltpu.VMEM((S, HV), BF16), pltpu.VMEM((...]
where the time goes in v4:
time: 137 us; the launch traced here: 136 us
  Pallas kernels  136 us (99%)
    pallas_call x1, Pallas kernels, shards(): pl.pallas_call(kernel, out_shape=(pltpu.VMEM((S, HV), BF16), pltpu.VMEM((...  133 us

profile of v4, /device:TPU:1, one launch (start us, length us, event | category | flops | bytes accessed | tf_op | source)
XLA Modules:
  0.0 136.5 jit_solution(10675973588459341879)
XLA Ops:
  0.6 133.1 %diloco.1 = (bf16[576,1024]{1,0:T(8,128)(2,1)S(1)}, bf16[512,4608]{1,0:T(8,128)(2,1)S(1)}, f32[18,1024]{1,0:T(8,128)S(1)}, f32[18,1024]{1,0:T(8,128)S(1)}) custom-call(bf16[576,1024]{1,0:T(8,128)(2,1)} %bitcast.7, bf16[512,4608]{1,0:T(8,128)(2,1)} %bitcast.5, bf16[512,1024]{1,0:T(8,128)(2,1)} %bitcast.9, f32[4608]{0:T(1024)} %gain.1, f32[18,1024]{1,0:T(8,128)} %glob.1, ...), custom_call_target="tpu_custom_call" | custom-call | flops 9663676416 | bytes 16777216 | tf_op jit(solution)/shard_map/diloco/pallas_call | solution.py:541
  133.8 2.7 %store.1 = (bf16[576,1024]{1,0:T(8,128)(2,1)}, bf16[512,4608]{1,0:T(8,128)(2,1)}, f32[18,1024]{1,0:T(8,128)}, f32[18,1024]{1,0:T(8,128)}) custom-call(bf16[576,1024]{1,0:T(8,128)(2,1)S(1)} %get-tuple-element.12.params, bf16[512,4608]{1,0:T(8,128)(2,1)S(1)} %get-tuple-element.13.tok, f32[18,1024]{1,0:T(8,128)S(1)} %get-tuple-element.14.glob, ...), custom_call_target="tpu_custom_call" | custom-call | tf_op jit(solution)/shard_map/store/pallas_call | solution.py:592

commit v5 on v4

--- a/solution.py
+++ b/solution.py
@@ -385,9 +385,11 @@
     def window(pos):
         return pl.ds(pl.multiple_of(lax.div(pos * OWN, 8) * 8, 8), WR)
 
-    def send_l(c, i):
+    def send_l(first, count, i):
         pos = lax.rem(zl + i // 2, 4) * 2 + lax.rem(core + i % 2, 2)
-        return remote(s8.at[c, window(pos)], lr.at[c, i], l_s, l_r, 2 + 7 * c + i, dev_l(i))
+        chunks = pl.ds(first, count)
+        sem = 2 + i + (7 if first else 0)
+        return remote(s8.at[chunks, window(pos)], lr.at[chunks, i], l_s, l_r, sem, dev_l(i))
 
     def update(c):
         send_g(1, c).wait_recv()
@@ -398,7 +400,7 @@
             grad = gk[1, c, :, part] + gr[1, c, :, part].astype(F32) + zr[c, :, part].astype(F32)
             now = (wg[1, pl.ds(w_rows, S), cols].astype(F32) - inner_rate * grad).astype(BF16)
             up[2 * c + k] = now
-        for i in range(1, 8):
+        for i in (4, 5, 2, 3, 6, 7, 1):
             send_y(c, i).start()
 
     def mix(c):
@@ -417,14 +419,23 @@
         for i in range(1, 8):
             total = total + yr[c, i].astype(F32)
         s8[c] = total
+
+    far_first = (4, 5, 2, 3, 6, 7, 1)
+
+    def start_l(first, count):
+        for i in far_first:
+            send_l(first, count, i).start()
+
+    def all_l(first, count):
         for i in range(1, 8):
-            send_l(c, i).start()
-
-    def all_l(c):
-        for i in range(1, 8):
-            send_l(c, i).wait_recv()
-        tot[2 * c + core] = s8[c, window(zl * 2 + core), :] + lr[c, 2] + lr[c, 4] + lr[c, 6]
-        tot[2 * c + 1 - core] = lr[c, 1] + lr[c, 3] + lr[c, 5] + lr[c, 7]
+            send_l(first, count, i).wait_recv()
+        for c in range(first, first + count):
+            tot[2 * c + core] = s8[c, window(zl * 2 + core), :] + lr[c, 2] + lr[c, 4] + lr[c, 6]
+            tot[2 * c + 1 - core] = lr[c, 1] + lr[c, 3] + lr[c, 5] + lr[c, 7]
+
+    def sent(*copies):
+        for cp in copies:
+            cp.wait_send()
 
     pass_on(0)
     pass_on(1)
@@ -446,6 +457,7 @@
     give(1)
     far_sum(3)
     dn(1, 0, put_xo)
+    sent(send_cot, send_w, send_prev, prev_l, *far_w, *send_n[:3])
     keep(1)
     for cp in forward:
         cp.wait_recv()
@@ -454,6 +466,11 @@
     for cp in send_x:
         cp.start()
     dn(0, 0, put_xo)
+    sent(send_n[3], *forward, *[send_g(0, c) for c in range(NC)])
+
+    @pl.when(edge)
+    def _():
+        sent(*relay)
 
     update(0)
     prev_to_y()
@@ -471,20 +488,23 @@
     send_x1.wait_recv()
     finish(0)
     mix(2)
+    finish(1)
+    finish(2)
+    sent(prev_c, send_x1, *prev_y, *[send_g(1, c) for c in range(NC)])
+    update(3)
     all_y(2)
-    finish(1)
-    update(3)
-    mix(3)
-    finish(2)
+    start_l(0, 3)
     finish(3)
     finish(4)
+    finish(5)
     all_y(3)
-    all_l(0)
-    all_l(1)
-    all_l(2)
-    finish(5)
+    start_l(3, 1)
+    mix(3)
     finish(6)
-    all_l(3)
+    finish(7)
+    sent(*send_x, *[send_s(c) for c in range(NC)], *[send_y(c, i) for c in range(NC) for i in range(1, 8)])
+    all_l(0, 3)
+    all_l(3, 1)
 
     place = lax.rem(zl, 2) * 2 + core
     for j in range(HV // 128):
@@ -498,23 +518,8 @@
         moved = nesterov * mom[:, cols] + delta
         new_momentum[:, cols] = moved
         new_global[:, cols] = glob[:, cols] - outer_rate * (delta + nesterov * moved)
-    finish(7)
-
-    for cp in [send_cot, send_w, send_prev, prev_c, send_x1, prev_l] + far_w + forward + send_n + send_x + prev_y:
-        cp.wait_send()
-
-    @pl.when(edge)
-    def _():
-        for cp in relay:
-            cp.wait_send()
-
-    for c in range(NC):
-        send_g(0, c).wait_send()
-        send_g(1, c).wait_send()
-        send_s(c).wait_send()
-        for i in range(1, 8):
-            send_y(c, i).wait_send()
-            send_l(c, i).wait_send()
+
+    sent(*[send_l(first, count, i) for first, count in ((0, 3), (3, 1)) for i in range(1, 8)])
 
 
 def store(params, tok, glob, mom, params_out, tokens_out, glob_out, mom_out, sems):
@@ -578,7 +583,7 @@
             dma((NZ + NC,)), dma((NZ + NC,)),
             dma((2,)), dma((2,)),
             dma((3 + 7 * NC,)), dma((3 + 7 * NC,)),
-            dma((3 + 7 * NC,)), dma((3 + 7 * NC,)),
+            dma((17,)), dma((17,)),
             dma((10,)),
         ],
         compiler_params=pltpu.CompilerParams(

time: 137 us -> 135 us (0.985)
  Pallas kernels: 136 us -> 134 us
    pallas_call x1, Pallas kernels: 133 us -> 131 us  [shards(): pl.pallas_call(kernel, out_shape=(pltpu.VMEM((S, HV), BF16), pltpu.VMEM((...]
where the time goes in v5:
time: 135 us; the launch traced here: 134 us
  Pallas kernels  134 us (99%)
    pallas_call x1, Pallas kernels, shards(): pl.pallas_call(kernel, out_shape=(pltpu.VMEM((S, HV), BF16), pltpu.VMEM((...  131 us

profile of v5, /device:TPU:1, one launch (start us, length us, event | category | flops | bytes accessed | tf_op | source)
XLA Modules:
  0.0 134.4 jit_solution(7829151226443259087)
XLA Ops:
  0.6 131.1 %diloco.1 = (bf16[576,1024]{1,0:T(8,128)(2,1)S(1)}, bf16[512,4608]{1,0:T(8,128)(2,1)S(1)}, f32[18,1024]{1,0:T(8,128)S(1)}, f32[18,1024]{1,0:T(8,128)S(1)}) custom-call(bf16[576,1024]{1,0:T(8,128)(2,1)} %bitcast.7, bf16[512,4608]{1,0:T(8,128)(2,1)} %bitcast.5, bf16[512,1024]{1,0:T(8,128)(2,1)} %bitcast.9, f32[4608]{0:T(1024)} %gain.1, f32[18,1024]{1,0:T(8,128)} %glob.1, ...), custom_call_target="tpu_custom_call" | custom-call | flops 9663676416 | bytes 16777216 | tf_op jit(solution)/shard_map/diloco/pallas_call | solution.py:546
  131.8 2.7 %store.1 = (bf16[576,1024]{1,0:T(8,128)(2,1)}, bf16[512,4608]{1,0:T(8,128)(2,1)}, f32[18,1024]{1,0:T(8,128)}, f32[18,1024]{1,0:T(8,128)}) custom-call(bf16[576,1024]{1,0:T(8,128)(2,1)S(1)} %get-tuple-element.12.params, bf16[512,4608]{1,0:T(8,128)(2,1)S(1)} %get-tuple-element.13.tok, f32[18,1024]{1,0:T(8,128)S(1)} %get-tuple-element.14.glob, ...), custom_call_target="tpu_custom_call" | custom-call | tf_op jit(solution)/shard_map/store/pallas_call | solution.py:597

commit v6 on v5

--- a/solution.py
+++ b/solution.py
@@ -325,11 +325,16 @@
                 ),
             )
 
+    def own_columns(o, at):
+        return pl.ds(pl.multiple_of(column(2 + o) + at, 128), 384)
+
     def put_xs(o, at, v):
-        xs[:, pl.ds(pl.multiple_of(o * Q + at, 128), 384)] = v.astype(BF16)
+        scaled = v * gv[:, own_columns(o, at)]
+        xs[:, pl.ds(pl.multiple_of(o * Q + at, 128), 384)] = scaled.astype(BF16)
 
     def put_xo(o, at, v):
-        xa[:, pl.ds(pl.multiple_of(column(2 + o) + at, 128), 384)] = v.astype(BF16)
+        scaled = v * gv[:, own_columns(o, at)]
+        xa[:, own_columns(o, at)] = scaled.astype(BF16)
 
     own_plane = pl.ds(Q, Q)
     send_x1 = remote(
@@ -352,18 +357,17 @@
 
             def parts(j):
                 cols = slice(j * 128, (j + 1) * 128)
-                unit = tok[rows, cols].astype(F32) * inv
-                return unit, gv[:, cols] * xa[rows, cols].astype(F32)
+                return tok[rows, cols].astype(F32), xa[rows, cols].astype(F32)
 
             acc = jnp.zeros((16, 128), F32)
             for j in range(D // 128):
-                unit, scaled = parts(j)
-                acc = acc + unit * scaled
-            mean = jnp.sum(acc, axis=-1, keepdims=True) * (1.0 / D)
+                v, scaled = parts(j)
+                acc = acc + v * scaled
+            weight = inv * inv * inv * (jnp.sum(acc, axis=-1, keepdims=True) * (1.0 / D))
 
             def result(j):
-                unit, scaled = parts(j)
-                return inv * (scaled - unit * mean)
+                v, scaled = parts(j)
+                return inv * scaled - weight * v
 
             def put(j, v):
                 tok[rows, j * 128 : (j + 1) * 128] = v.astype(BF16)
@@ -380,7 +384,7 @@
     def send_y(c, i):
         rows = pl.ds(pl.multiple_of(lax.rem(y + i // 2, 4) * YR, 16), YR)
         src = up.at[2 * c + lax.rem(core + i % 2, 2), rows]
-        return remote(src, yr.at[c, i], y_s, y_r, 2 + 7 * c + i, dev_y(i))
+        return remote(src, yr.at[c, i], y_s, y_r, 3 + c, dev_y(i))
 
     def window(pos):
         return pl.ds(pl.multiple_of(lax.div(pos * OWN, 8) * 8, 8), WR)
@@ -388,8 +392,17 @@
     def send_l(first, count, i):
         pos = lax.rem(zl + i // 2, 4) * 2 + lax.rem(core + i % 2, 2)
         chunks = pl.ds(first, count)
-        sem = 2 + i + (7 if first else 0)
+        sem = 4 if first else 3
         return remote(s8.at[chunks, window(pos)], lr.at[chunks, i], l_s, l_r, sem, dev_l(i))
+
+    def all_of(ref, sem):
+        pltpu.make_async_copy(ref, ref, sem).wait()
+
+    def seven_y(c, sems):
+        all_of(yr.at[c, pl.ds(1, 7)], sems.at[3 + c])
+
+    def seven_l(first, count, sems):
+        all_of(lr.at[pl.ds(first, count), pl.ds(1, 7)], sems.at[4 if first else 3])
 
     def update(c):
         send_g(1, c).wait_recv()
@@ -413,8 +426,7 @@
             ).astype(BF16)
 
     def all_y(c):
-        for i in range(1, 8):
-            send_y(c, i).wait_recv()
+        seven_y(c, y_r)
         total = up[2 * c + core, y_rows, :].astype(F32)
         for i in range(1, 8):
             total = total + yr[c, i].astype(F32)
@@ -427,8 +439,7 @@
             send_l(first, count, i).start()
 
     def all_l(first, count):
-        for i in range(1, 8):
-            send_l(first, count, i).wait_recv()
+        seven_l(first, count, l_r)
         for c in range(first, first + count):
             tot[2 * c + core] = s8[c, window(zl * 2 + core), :] + lr[c, 2] + lr[c, 4] + lr[c, 6]
             tot[2 * c + 1 - core] = lr[c, 1] + lr[c, 3] + lr[c, 5] + lr[c, 7]
@@ -502,7 +513,9 @@
     mix(3)
     finish(6)
     finish(7)
-    sent(*send_x, *[send_s(c) for c in range(NC)], *[send_y(c, i) for c in range(NC) for i in range(1, 8)])
+    sent(*send_x, *[send_s(c) for c in range(NC)])
+    for c in range(NC):
+        seven_y(c, y_s)
     all_l(0, 3)
     all_l(3, 1)
 
@@ -519,7 +532,8 @@
         new_momentum[:, cols] = moved
         new_global[:, cols] = glob[:, cols] - outer_rate * (delta + nesterov * moved)
 
-    sent(*[send_l(first, count, i) for first, count in ((0, 3), (3, 1)) for i in range(1, 8)])
+    seven_l(0, 3, l_s)
+    seven_l(3, 1, l_s)
 
 
 def store(params, tok, glob, mom, params_out, tokens_out, glob_out, mom_out, sems):
@@ -582,8 +596,8 @@
             dma((5 + 2 * NC,)), dma((5 + 2 * NC,)),
             dma((NZ + NC,)), dma((NZ + NC,)),
             dma((2,)), dma((2,)),
-            dma((3 + 7 * NC,)), dma((3 + 7 * NC,)),
-            dma((17,)), dma((17,)),
+            dma((3 + NC,)), dma((3 + NC,)),
+            dma((5,)), dma((5,)),
             dma((10,)),
         ],
         compiler_params=pltpu.CompilerParams(

time: 135 us -> 134 us (level)
  no operation moved by 1% of the time
where the time goes in v6:
time: 134 us
  Pallas kernels  133 us (99%)
    pallas_call x1, Pallas kernels, shards(): pl.pallas_call(kernel, out_shape=(pltpu.VMEM((S, HV), BF16), pltpu.VMEM((...  130 us

profile of v6, /device:TPU:1, one launch (start us, length us, event | category | flops | bytes accessed | tf_op | source)
XLA Modules:
  0.0 133.8 jit_solution(8887927427448818692)
XLA Ops:
  0.6 130.5 %diloco.1 = (bf16[576,1024]{1,0:T(8,128)(2,1)S(1)}, bf16[512,4608]{1,0:T(8,128)(2,1)S(1)}, f32[18,1024]{1,0:T(8,128)S(1)}, f32[18,1024]{1,0:T(8,128)S(1)}) custom-call(bf16[576,1024]{1,0:T(8,128)(2,1)} %bitcast.7, bf16[512,4608]{1,0:T(8,128)(2,1)} %bitcast.5, bf16[512,1024]{1,0:T(8,128)(2,1)} %bitcast.9, f32[4608]{0:T(1024)} %gain.1, f32[18,1024]{1,0:T(8,128)} %glob.1, ...), custom_call_target="tpu_custom_call" | custom-call | flops 9663676416 | bytes 16777216 | tf_op jit(solution)/shard_map/diloco/pallas_call | solution.py:560
  131.1 2.7 %store.1 = (bf16[576,1024]{1,0:T(8,128)(2,1)}, bf16[512,4608]{1,0:T(8,128)(2,1)}, f32[18,1024]{1,0:T(8,128)}, f32[18,1024]{1,0:T(8,128)}) custom-call(bf16[576,1024]{1,0:T(8,128)(2,1)S(1)} %get-tuple-element.12.params, bf16[512,4608]{1,0:T(8,128)(2,1)S(1)} %get-tuple-element.13.tok, f32[18,1024]{1,0:T(8,128)S(1)} %get-tuple-element.14.glob, ...), custom_call_target="tpu_custom_call" | custom-call | tf_op jit(solution)/shard_map/store/pallas_call | solution.py:611

commit v7 on v6

--- a/solution.py
+++ b/solution.py
@@ -297,13 +297,15 @@
         def _(c):
             gk[o, c] = product(o, my_rows, c)
 
-    def send_s(c):
-        return remote(zs.at[c], zr.at[c], z_s, z_r, NZ + c, dev_z)
+    def send_s(c, h):
+        rows = pl.ds(h * (S // 2), S // 2) if c == NC - 1 else pl.ds(0, S)
+        return remote(zs.at[c, rows], zr.at[c, rows], z_s, z_r, NZ + c + h, dev_z)
 
     def far_sum(c):
         send_g(0, c).wait_recv()
         zs[c] = (gk[0, c] + gr[0, c].astype(F32)).astype(BF16)
-        send_s(c).start()
+        for h in range(2 if c == NC - 1 else 1):
+            send_s(c, h).start()
 
     def wrap(o):
         @pl.when(base == 64)
@@ -406,15 +408,25 @@
 
     def update(c):
         send_g(1, c).wait_recv()
-        send_s(c).wait_recv()
-        for k in range(2):
-            part = slice(k * 128, (k + 1) * 128)
-            cols = slice(c * CW + k * 128, c * CW + (k + 1) * 128)
-            grad = gk[1, c, :, part] + gr[1, c, :, part].astype(F32) + zr[c, :, part].astype(F32)
-            now = (wg[1, pl.ds(w_rows, S), cols].astype(F32) - inner_rate * grad).astype(BF16)
-            up[2 * c + k] = now
-        for i in (4, 5, 2, 3, 6, 7, 1):
-            send_y(c, i).start()
+        halves = 2 if c == NC - 1 else 1
+        for h in range(halves):
+            send_s(c, h).wait_recv()
+            rows = slice(h * (S // 2), (h + 1) * (S // 2)) if halves == 2 else slice(0, S)
+            w_here = pl.ds(pl.multiple_of(w_rows + rows.start, 16), rows.stop - rows.start)
+            for k in range(2):
+                part = slice(k * 128, (k + 1) * 128)
+                cols = slice(c * CW + k * 128, c * CW + (k + 1) * 128)
+                grad = gk[1, c, rows, part] + gr[1, c, rows, part].astype(F32) + zr[c, rows, part].astype(F32)
+                now = (wg[1, w_here, cols].astype(F32) - inner_rate * grad).astype(BF16)
+                up[2 * c + k, rows] = now
+            for i in (4, 5, 2, 3, 6, 7, 1):
+                if halves == 1:
+                    send_y(c, i).start()
+                else:
+
+                    @pl.when(lax.div(lax.rem(y + i // 2, 4), 2) == h)
+                    def _():
+                        send_y(c, i).start()
 
     def mix(c):
         for k in range(2):
@@ -513,7 +525,7 @@
     mix(3)
     finish(6)
     finish(7)
-    sent(*send_x, *[send_s(c) for c in range(NC)])
+    sent(*send_x, *[send_s(c, 0) for c in range(NC)], send_s(NC - 1, 1))
     for c in range(NC):
         seven_y(c, y_s)
     all_l(0, 3)
@@ -594,7 +606,7 @@
             pltpu.VMEM((2, S, HV // 2), BF16),
             dma((6 + NT,)), dma((6 + NT,)),
             dma((5 + 2 * NC,)), dma((5 + 2 * NC,)),
-            dma((NZ + NC,)), dma((NZ + NC,)),
+            dma((NZ + NC + 1,)), dma((NZ + NC + 1,)),
             dma((2,)), dma((2,)),
             dma((3 + NC,)), dma((3 + NC,)),
             dma((5,)), dma((5,)),

time: 134 us -> 134 us (level)
  no operation moved by 1% of the time
where the time goes in v7:
time: 134 us; the launch traced here: 133 us
  Pallas kernels  133 us (99%)
    pallas_call x1, Pallas kernels, shards(): pl.pallas_call(kernel, out_shape=(pltpu.VMEM((S, HV), BF16), pltpu.VMEM((...  130 us

profile of v7, /device:TPU:1, one launch (start us, length us, event | category | flops | bytes accessed | tf_op | source)
XLA Modules:
  0.0 133.5 jit_solution(11723337323435211591)
XLA Ops:
  0.6 130.2 %diloco.1 = (bf16[576,1024]{1,0:T(8,128)(2,1)S(1)}, bf16[512,4608]{1,0:T(8,128)(2,1)S(1)}, f32[18,1024]{1,0:T(8,128)S(1)}, f32[18,1024]{1,0:T(8,128)S(1)}) custom-call(bf16[576,1024]{1,0:T(8,128)(2,1)} %bitcast.7, bf16[512,4608]{1,0:T(8,128)(2,1)} %bitcast.5, bf16[512,1024]{1,0:T(8,128)(2,1)} %bitcast.9, f32[4608]{0:T(1024)} %gain.1, f32[18,1024]{1,0:T(8,128)} %glob.1, ...), custom_call_target="tpu_custom_call" | custom-call | flops 9663676416 | bytes 16777216 | tf_op jit(solution)/shard_map/diloco/pallas_call | solution.py:572
  130.8 2.7 %store.1 = (bf16[576,1024]{1,0:T(8,128)(2,1)}, bf16[512,4608]{1,0:T(8,128)(2,1)}, f32[18,1024]{1,0:T(8,128)}, f32[18,1024]{1,0:T(8,128)}) custom-call(bf16[576,1024]{1,0:T(8,128)(2,1)S(1)} %get-tuple-element.12.params, bf16[512,4608]{1,0:T(8,128)(2,1)S(1)} %get-tuple-element.13.tok, f32[18,1024]{1,0:T(8,128)S(1)} %get-tuple-element.14.glob, ...), custom_call_target="tpu_custom_call" | custom-call | tf_op jit(solution)/shard_map/store/pallas_call | solution.py:623
